TPU v7x, 128 devices: a whole 4x4x4 slice. The times are simulated.
128 devices in a mesh: gx: 16 (over z, x_lo, core), gy: 8 (over y, x_hi).
Axes of the slice: x: 4 (x_hi: 2, x_lo: 2; x = x_hi * 2 + x_lo), y: 4, z: 4, core: 2. Of those that a mesh axis runs over, the one named last changes fastest.
Arguments:
- density: float32 [512, 512, 512], P('gx', 'gy'), may hold values from -6 to 6
- radius_cells: int32 [2], replicated, may hold values from 1 to 32
Outputs:
- filtered: float32 [2, 512, 512, 512], P(None, 'gx', 'gy')
All inputs are finite; a program needn't handle non-finite values.
Results may differ from a plain program's by a relative error of at most 0.0001.
Values sent between devices are 32-bit elements; how exact they have to be, the bound alone decides.
No kernel may reach another device: no remote copies, remote signals or barrier semaphores. Data moves between devices by JAX's collectives and lax.ppermute only.
A program may use at most 128 MiB of HBM per device.

v0:
```python
import math

import jax
import jax.numpy as jnp
from jax import lax
from jax.sharding import PartitionSpec as P

HIGHEST = lax.Precision.HIGHEST


def window(u_value):
    is_small = u_value < 0.2
    safe_u = jnp.where(is_small, 1.0, u_value)
    closed_form = 3.0 * (jnp.sin(safe_u) - safe_u * jnp.cos(safe_u)) / (safe_u * safe_u * safe_u)
    series = 1.0 - u_value * u_value / 10.0 + u_value**4 / 280.0
    return jnp.where(is_small, series, closed_form)


def dft_tables(length, direction):
    indices = jnp.arange(length, dtype=jnp.int32)
    product = indices[:, None] * indices[None, :] % length
    angles = 2.0 * math.pi / length * product.astype(jnp.float32)
    return (jnp.cos(angles), direction * jnp.sin(angles))


def twiddle_table(length, quarter, direction):
    row_ids = jnp.arange(4, dtype=jnp.int32)[:, None]
    col_ids = jnp.arange(quarter, dtype=jnp.int32)[None, :]
    angles = 2.0 * math.pi / length * (row_ids * col_ids % length).astype(jnp.float32)
    return (jnp.cos(angles), direction * jnp.sin(angles))


def product_section(real_part, imag_part, joined_form, cos_table, sin_table):
    block_table = jnp.stack(
        [jnp.stack([cos_table, sin_table], 1), jnp.stack([-sin_table, cos_table], 1)], 0
    )
    stacked = jnp.stack([real_part, imag_part], 0)
    result = jnp.einsum(
        joined_form, stacked, block_table, precision=HIGHEST, preferred_element_type=jnp.float32
    )
    return (result[0], result[1])


def rotate(real_part, imag_part, cos_table, sin_table):
    return (
        real_part * cos_table - imag_part * sin_table,
        real_part * sin_table + imag_part * cos_table,
    )


def radix_four(real_part, imag_part, along_axis, direction):
    reals = [lax.index_in_dim(real_part, offset, along_axis, keepdims=False) for offset in range(4)]
    imags = [lax.index_in_dim(imag_part, offset, along_axis, keepdims=False) for offset in range(4)]
    sum_even_re = reals[0] + reals[2]
    sum_even_im = imags[0] + imags[2]
    diff_even_re = reals[0] - reals[2]
    diff_even_im = imags[0] - imags[2]
    sum_odd_re = reals[1] + reals[3]
    sum_odd_im = imags[1] + imags[3]
    diff_odd_re = reals[1] - reals[3]
    diff_odd_im = imags[1] - imags[3]
    out_re = [
        sum_even_re + sum_odd_re,
        diff_even_re - direction * diff_odd_im,
        sum_even_re - sum_odd_re,
        diff_even_re + direction * diff_odd_im,
    ]
    out_im = [
        sum_even_im + sum_odd_im,
        diff_even_im + direction * diff_odd_re,
        sum_even_im - sum_odd_im,
        diff_even_im - direction * diff_odd_re,
    ]
    return (jnp.stack(out_re, along_axis), jnp.stack(out_im, along_axis))


def signed_squares(values, length):
    signed = jnp.where(values > length // 2, values - length, values).astype(jnp.float32)
    return signed * signed


def per_device(density, radius_cells):
    rows_x, rows_y, length = density.shape
    quarter = length // 4
    count_gx = lax.axis_size("gx")
    count_gy = lax.axis_size("gy")
    devices = count_gx * count_gy
    slab_rows = rows_x // count_gy
    band_rows = length // devices
    fwd_cos, fwd_sin = dft_tables(quarter, -1.0)
    inv_cos, inv_sin = dft_tables(quarter, 1.0)
    twid_fwd_cos, twid_fwd_sin = twiddle_table(length, quarter, -1.0)
    twid_inv_cos, twid_inv_sin = twiddle_table(length, quarter, 1.0)
    scale_factor = 1.0 / float(length) ** 3
    real_part = density.reshape(rows_x, rows_y, 4, quarter)
    imag_part = jnp.zeros_like(real_part)
    real_part, imag_part = radix_four(real_part, imag_part, 2, -1.0)
    real_part, imag_part = rotate(real_part, imag_part, twid_fwd_cos, twid_fwd_sin)
    real_part, imag_part = product_section(
        real_part, imag_part, "pxyab,pbqc->qxyac", fwd_cos, fwd_sin
    )
    part_re = lax.all_to_all(real_part, "gy", split_axis=0, concat_axis=1, tiled=True)
    part_im = lax.all_to_all(imag_part, "gy", split_axis=0, concat_axis=1, tiled=True)
    piece_rows = part_re.shape[0]
    slices = part_re.shape[2]
    shaped = (piece_rows, 4, quarter, slices, quarter)
    part_re = part_re.reshape(shaped)
    part_im = part_im.reshape(shaped)
    part_re, part_im = radix_four(part_re, part_im, 1, -1.0)
    part_re, part_im = rotate(
        part_re, part_im, twid_fwd_cos[None, :, :, None, None], twid_fwd_sin[None, :, :, None, None]
    )
    part_re, part_im = product_section(part_re, part_im, "piabcd,pbqe->qiaecd", fwd_cos, fwd_sin)
    flat_shape = (piece_rows, length, slices, quarter)
    real_part = part_re.reshape(flat_shape)
    imag_part = part_im.reshape(flat_shape)
    real_part = real_part.reshape(slab_rows, length, length)
    imag_part = imag_part.reshape(slab_rows, length, length)
    trail = real_part.shape[-1]
    moved_re, moved_im = (
        lax.all_to_all(real_part[None], ("gx", "gy"), split_axis=2, concat_axis=0, tiled=True),
        lax.all_to_all(imag_part[None], ("gx", "gy"), split_axis=2, concat_axis=0, tiled=True),
    )
    x_shape = (4, quarter, band_rows, trail)
    real_part = moved_re.reshape(x_shape)
    imag_part = moved_im.reshape(x_shape)
    real_part, imag_part = radix_four(real_part, imag_part, 0, -1.0)
    real_part, imag_part = rotate(
        real_part, imag_part, twid_fwd_cos[:, :, None, None], twid_fwd_sin[:, :, None, None]
    )
    real_part, imag_part = product_section(
        real_part, imag_part, "pabcd,pbqe->qaecd", fwd_cos, fwd_sin
    )
    pair_freq = (
        jnp.arange(4, dtype=jnp.int32)[:, None] + 4 * jnp.arange(quarter, dtype=jnp.int32)[None, :]
    )
    pair_squares = signed_squares(pair_freq, length)
    flat_band = lax.axis_index(("gx", "gy")) * band_rows + jnp.arange(band_rows, dtype=jnp.int32)
    band_freq = flat_band // quarter + 4 * (flat_band % quarter)
    band_squares = signed_squares(band_freq, length)
    trail_ids = jnp.arange(trail, dtype=jnp.int32)
    trail_freq = trail_ids // quarter + 4 * (trail_ids % quarter)
    trail_squares = signed_squares(trail_freq, length)
    k_squared = (
        pair_squares[:, :, None, None]
        + band_squares[None, None, :, None]
        + trail_squares[None, None, None, :]
    )
    k_length = 2.0 * math.pi / length * jnp.sqrt(k_squared)
    radius_values = radius_cells.astype(jnp.float32)
    weight_first = window(k_length * radius_values[0])
    weight_second = window(k_length * radius_values[1])
    packed_re = real_part * weight_first - imag_part * weight_second
    packed_im = imag_part * weight_first + real_part * weight_second
    rest = packed_re.shape[-1]
    packed_re, packed_im = product_section(
        packed_re, packed_im, "pabcd,pbqe->qaecd", inv_cos, inv_sin
    )
    packed_re, packed_im = rotate(
        packed_re, packed_im, twid_inv_cos[:, :, None, None], twid_inv_sin[:, :, None, None]
    )
    packed_re, packed_im = radix_four(packed_re, packed_im, 0, 1.0)
    flat_x = (length, band_rows, rest)
    back_re, back_im = (
        lax.all_to_all(
            packed_re.reshape(flat_x), ("gx", "gy"), split_axis=0, concat_axis=1, tiled=True
        ),
        lax.all_to_all(
            packed_im.reshape(flat_x), ("gx", "gy"), split_axis=0, concat_axis=1, tiled=True
        ),
    )
    y_shape = (slab_rows, 4, quarter, rest)
    packed_re = back_re.reshape(y_shape)
    packed_im = back_im.reshape(y_shape)
    packed_re, packed_im = product_section(
        packed_re, packed_im, "piabr,pbqe->qiaer", inv_cos, inv_sin
    )
    packed_re, packed_im = rotate(
        packed_re, packed_im, twid_inv_cos[None, :, :, None], twid_inv_sin[None, :, :, None]
    )
    packed_re, packed_im = radix_four(packed_re, packed_im, 1, 1.0)
    flat_y = (slab_rows, length, rest)
    packed_re, packed_im = (
        lax.all_to_all(packed_re.reshape(flat_y), "gy", split_axis=1, concat_axis=0, tiled=True),
        lax.all_to_all(packed_im.reshape(flat_y), "gy", split_axis=1, concat_axis=0, tiled=True),
    )
    z_shape = (rows_x, rows_y, 4, quarter)
    packed_re = packed_re.reshape(z_shape)
    packed_im = packed_im.reshape(z_shape)
    packed_re, packed_im = product_section(
        packed_re, packed_im, "pxyab,pbqc->qxyac", inv_cos, inv_sin
    )
    packed_re, packed_im = rotate(packed_re, packed_im, twid_inv_cos, twid_inv_sin)
    packed_re, packed_im = radix_four(packed_re, packed_im, 2, 1.0)
    field_first = packed_re.reshape(rows_x, rows_y, length) * scale_factor
    field_second = packed_im.reshape(rows_x, rows_y, length) * scale_factor
    return jnp.stack([field_first, field_second])


def solution(mesh):
    return jax.shard_map(
        per_device,
        mesh=mesh,
        in_specs=(P("gx", "gy", None), P()),
        out_specs=P(None, "gx", "gy", None),
        check_vma=False,
    )
```

profile of v0, /device:TPU:1, one launch (start us, length us, event | category | flops | bytes accessed | tf_op | source)
XLA Modules:
  0.0 730.1 jit_solution(4366535285669883104)
XLA Ops:
  0.9 5.2 reshape.1656
  6.1 10.9 %fusion.121 = (f32[32,64,1,128]{3,2,1,0:T(1,128)S(1)}, f32[32,64,1,128]{3,2,1,0:T(1,128)S(1)}, f32[32,64,1,128]{3,2,1,0:T(1,128)S(1)}, f32[32,64,1,128]{3,2,1,0:T(1,128)S(1)}) fusion(f32[32,64,4,128]{3,2,1,0:T(4,128)} %reshape.1656), kind=kLoop, calls=%fused_computation.258 | loop fusion | bytes 8388608 | tf_op jit(solution)/shard_map/slice | solution.py:52
  19.9 8.2 %fusion.33 = f32[2,32,64,4,128]{4,2,3,1,0:T(8,128)S(1)} fusion(f32[1,32,64,4,128]{4,2,0,3,1:T(8,128)S(1)} %get-tuple-element.42, f32[1,32,64,4,128]{4,2,0,3,1:T(8,128)S(1)} %get-tuple-element.41, f32[1,128,2,128]{3,1,0,2:T(8,128)S(1)} %get-tuple-element.73, f32[1,128,2,128]{3,1,0,2:T(8,128)S(1)} %get-tuple-element.74), kind=kOutput, calls=%fused_computation.79 | convolution fusion | flops 6444613632 | bytes 17039360 | tf_op jit(solution)/shard_map/pxyab,pbqc->qxyac/dot_general | solution.py:38
  28.1 3.3 slice_bitcast_fusion.7
  31.4 57.4 %all_to_all.120 = f32[32,64,4,128]{3,1,2,0:T(8,128)} all-to-all(f32[32,64,4,128]{3,1,2,0:T(8,128)S(1)} %get-tuple-element.39), channel_id=1, replica_groups=mesh['gx'=16,'gy'=8] {'gy'}, dimensions={0} | all-to-all | bytes 8388608 | tf_op jit(solution)/shard_map/all_to_all | solution.py:102
  88.8 4.6 all-to-all-start.1
  93.3 4.8 copy.134
  98.2 44.3 %all-to-all-done.1 = f32[32,64,4,128]{3,1,2,0:T(8,128)} async-done(((f32[32,64,4,128]{3,1,2,0:T(8,128)}), f32[32,64,4,128]{3,1,2,0:T(8,128)}, u32[]{:S(2)}, u32[]{:S(2)}) %all-to-all-start.1) | async-done | bytes 4194336 | tf_op jit(solution)/shard_map/all_to_all | solution.py:103
  142.4 2.7 copy.139
  149.9 8.9 %fusion.32 = f32[2,4,4,128,4,128]{5,3,4,2,1,0:T(8,128)S(1)} fusion(f32[1,4,4,128,4,128]{5,3,0,4,2,1:T(8,128)S(1)} %get-tuple-element.16, f32[1,4,4,128,4,128]{5,3,0,4,2,1:T(8,128)S(1)} %get-tuple-element.15, f32[1,128,2,128]{3,1,0,2:T(8,128)S(1)} %get-tuple-element.73, f32[1,128,2,128]{3,1,0,2:T(8,128)S(1)} %get-tuple-element.74), kind=kOutput, calls=%fused_computation.78 | convolution fusion | flops 6444613632 | bytes 17039360 | tf_op jit(solution)/shard_map/piabcd,pbqe->qiaecd/dot_general | solution.py:38
  158.8 2.9 fusion.120
  161.6 2.8 copy.150
  164.4 15.1 %copy.151 = f32[1,4,512,512]{3,0,1,2:T(1,128)} copy(f32[1,4,512,512]{3,0,2,1:T(1,128)S(1)} %bitcast.352) | data formatting | bytes 8388608 | tf_op jit(solution)/shard_map/broadcast_in_dim;reshape;reshape;squeeze | solution.py:121
  179.5 9.7 %all-to-all-start.2 = ((f32[1,4,512,512]{3,0,1,2:T(1,128)}), f32[1,4,512,512]{3,0,1,2:T(1,128)}, u32[]{:S(2)}, u32[]{:S(2)}) async-start(f32[1,4,512,512]{3,0,1,2:T(1,128)} %copy.151), calls=%async_computation.2 | async-start | bytes 8388608 | tf_op jit(solution)/shard_map/all_to_all | solution.py:121
  189.2 5.0 copy.153
  194.2 4.9 copy.154
  199.1 42.6 %all-to-all-done.2 = f32[1,4,512,512]{3,0,1,2:T(1,128)} async-done(((f32[1,4,512,512]{3,0,1,2:T(1,128)}), f32[1,4,512,512]{3,0,1,2:T(1,128)}, u32[]{:S(2)}, u32[]{:S(2)}) %all-to-all-start.2) | async-done | bytes 4194336 | tf_op jit(solution)/shard_map/all_to_all | solution.py:121
  241.6 5.5 all-to-all-start.3
  249.9 3.3 copy.205
  257.4 42.3 %all-to-all-done.3 = f32[1,4,512,512]{3,0,1,2:T(1,128)} async-done(((f32[1,4,512,512]{3,0,1,2:T(1,128)}), f32[1,4,512,512]{3,0,1,2:T(1,128)}, u32[]{:S(2)}, u32[]{:S(2)}) %all-to-all-start.3) | async-done | bytes 4194336 | tf_op jit(solution)/shard_map/all_to_all | solution.py:122
  299.7 3.4 copy.206
  308.5 2.6 stack.262
  313.4 2.7 stack.261
  320.7 2.7 stack.263
  324.4 2.6 stack.264
  331.2 2.4 copy.160
  333.6 2.7 stack.268
  337.3 2.7 stack.269
  347.7 8.9 %fusion.31 = f32[2,4,128,4,512]{4,2,3,1,0:T(8,128)S(1)} fusion(f32[1,4,128,4,512]{4,2,0,3,1:T(8,128)S(1)} %get-tuple-element.14, f32[1,4,128,4,512]{4,2,0,3,1:T(8,128)S(1)} %get-tuple-element.13, f32[1,128,2,128]{3,1,0,2:T(8,128)S(1)} %get-tuple-element.73, f32[1,128,2,128]{3,1,0,2:T(8,128)S(1)} %copy-done.15), kind=kOutput, calls=%fused_computation.77 | convolution fusion | flops 6444613632 | bytes 17039360 | tf_op jit(solution)/shard_map/pabcd,pbqe->qaecd/dot_general | solution.py:38
  356.6 36.2 %multiply_subtract_fusion.3 = (f32[1,4,128,4,512]{4,2,3,1,0:T(8,128)S(1)}, f32[1,4,128,4,512]{4,2,3,1,0:T(8,128)S(1)}) fusion(f32[2,4,128,4,512]{4,2,3,1,0:T(8,128)S(1)} %fusion.31, f32[]{:T(128)} %bitcast.58, f32[512]{0:T(512)S(1)} %fusion.104, f32[4,128,4]{1,2,0:T(4,128)S(1)} %copy-done.16, f32[]{:T(128)} %bitcast.60), kind=kLoop, calls=%fused_computation.66 | loop fusion | flops 40894464 | bytes 16787464 | tf_op jit(solution)/shard_map/sub | solution.py:153
  392.8 8.5 %fusion.26 = f32[2,4,128,4,512]{4,2,3,1,0:T(8,128)S(1)} fusion(f32[1,4,128,4,512]{4,2,3,1,0:T(8,128)S(1)} %get-tuple-element.6, f32[1,4,128,4,512]{4,2,3,1,0:T(8,128)S(1)} %get-tuple-element.5, f32[1,128,2,128]{3,1,2,0:T(8,128)S(1)} %get-tuple-element.75, f32[1,128,2,128]{3,1,2,0:T(8,128)S(1)} %get-tuple-element.72), kind=kOutput, calls=%fused_computation.74 | convolution fusion | flops 6444613632 | bytes 17039360 | tf_op jit(solution)/shard_map/pabcd,pbqe->qaecd/dot_general | solution.py:38
  406.3 4.7 copy.166
  411.0 5.5 all-to-all-start.4
  416.5 2.8 fusion.48
  420.3 4.7 copy.169
  425.0 44.0 %all-to-all-done.4 = f32[512,4,512]{2,1,0:T(4,128)} async-done(((f32[512,4,512]{2,1,0:T(4,128)}), f32[512,4,512]{2,1,0:T(4,128)}, u32[]{:S(2)}, u32[]{:S(2)}) %all-to-all-start.4) | async-done | bytes 4194336 | tf_op jit(solution)/shard_map/all_to_all | solution.py:165
  469.1 6.1 all-to-all-start.5
  475.1 5.1 copy.167
  480.2 5.4 stack_reshape.12
  485.6 42.0 %all-to-all-done.5 = f32[512,4,512]{2,1,0:T(4,128)} async-done(((f32[512,4,512]{2,1,0:T(4,128)}), f32[512,4,512]{2,1,0:T(4,128)}, u32[]{:S(2)}, u32[]{:S(2)}) %all-to-all-start.5) | async-done | bytes 4194336 | tf_op jit(solution)/shard_map/all_to_all | solution.py:168
  527.5 5.0 copy.170
  532.6 5.3 stack_reshape.13
  537.9 12.4 %fusion.30 = f32[2,4,4,128,512]{4,3,2,1,0:T(8,128)S(1)} fusion(f32[1,4,4,128,512]{4,3,0,2,1:T(8,128)} %stack_reshape.13, f32[1,4,4,128,512]{4,3,0,2,1:T(8,128)} %stack_reshape.12, f32[1,128,2,128]{3,1,2,0:T(8,128)S(1)} %get-tuple-element.75, f32[1,128,2,128]{3,1,2,0:T(8,128)S(1)} %get-tuple-element.72), kind=kOutput, calls=%fused_computation.76 | convolution fusion | flops 6444613632 | bytes 17039360 | tf_op jit(solution)/shard_map/piabr,pbqe->qiaer/dot_general | solution.py:38
  554.9 4.7 copy.172
  559.6 4.6 all-to-all-start.6
  564.2 2.8 fusion.56
  567.4 4.7 copy.175
  572.1 42.1 %all-to-all-done.6 = f32[4,512,512]{2,0,1:T(4,128)} async-done(((f32[4,512,512]{2,0,1:T(4,128)}), f32[4,512,512]{2,0,1:T(4,128)}, u32[]{:S(2)}, u32[]{:S(2)}) %all-to-all-start.6) | async-done | bytes 4194336 | tf_op jit(solution)/shard_map/all_to_all | solution.py:184
  614.2 4.8 all-to-all-start.7
  619.0 3.5 copy.173
  622.6 2.6 copy.174
  625.2 5.3 stack_reshape.14
  630.5 4.8 copy.178
  635.3 32.7 %all-to-all-done.7 = f32[4,512,512]{2,0,1:T(4,128)} async-done(((f32[4,512,512]{2,0,1:T(4,128)}), f32[4,512,512]{2,0,1:T(4,128)}, u32[]{:S(2)}, u32[]{:S(2)}) %all-to-all-start.7) | async-done | bytes 4194336 | tf_op jit(solution)/shard_map/all_to_all | solution.py:185
  668.1 3.5 copy.176
  671.6 2.6 copy.177
  674.2 5.3 stack_reshape.15
  679.4 3.0 copy.179
  682.9 8.4 %fusion.29 = f32[2,32,64,4,128]{4,2,3,1,0:T(8,128)S(1)} fusion(f32[1,32,64,4,128]{4,2,0,3,1:T(8,128)S(1)} %copy.179, f32[1,32,64,4,128]{4,2,0,3,1:T(8,128)S(1)} %copy-done.5, f32[1,128,2,128]{3,1,2,0:T(8,128)S(1)} %get-tuple-element.75, f32[1,128,2,128]{3,1,2,0:T(8,128)S(1)} %get-tuple-element.72), kind=kOutput, calls=%fused_computation.75 | convolution fusion | flops 6444613632 | bytes 17039360 | tf_op jit(solution)/shard_map/pxyab,pbqc->qxyac/dot_general | solution.py:38
  697.1 5.6 copy.181
  702.7 5.5 mul.1171
  709.8 5.6 copy.182
  715.4 5.6 mul.1173
  721.0 8.7 %pad_maximum_fusion.1 = f32[2,32,64,512]{3,2,1,0:T(8,128)} fusion(f32[1,32,64,512]{3,2,1,0:T(8,128)} %mul.1173, f32[1,32,64,512]{3,2,1,0:T(8,128)} %mul.1171), kind=kLoop, calls=%fused_computation.21 | loop fusion | flops 2097152 | bytes 16777216 | tf_op jit(solution)/shard_map/stack | solution.py:197
  (95 shorter events, 59.5 us)
Async XLA Ops:
  18.1 131.9 %copy-start.14 = (f32[1,128,2,128]{3,1,0,2:T(8,128)}, f32[1,128,2,128]{3,1,0,2:T(8,128)S(1)}, u32[]{:S(2)}) copy-start(f32[1,128,2,128]{3,1,0,2:T(8,128)S(1)} %get-tuple-element.74) | copy-start | bytes 393220
  88.8 53.7 %all-to-all-start.1 = ((f32[32,64,4,128]{3,1,2,0:T(8,128)}), f32[32,64,4,128]{3,1,2,0:T(8,128)}, u32[]{:S(2)}, u32[]{:S(2)}) async-start(f32[32,64,4,128]{3,1,2,0:T(8,128)} %get-tuple-element.40), calls=%async_computation.1 | async-start | bytes 8388608 | tf_op jit(solution)/shard_map/all_to_all | solution.py:103
  142.4 3.4 copy-start.2
  179.5 62.1 %all-to-all-start.2 = ((f32[1,4,512,512]{3,0,1,2:T(1,128)}), f32[1,4,512,512]{3,0,1,2:T(1,128)}, u32[]{:S(2)}, u32[]{:S(2)}) async-start(f32[1,4,512,512]{3,0,1,2:T(1,128)} %copy.151), calls=%async_computation.2 | async-start | bytes 8388608 | tf_op jit(solution)/shard_map/all_to_all | solution.py:121
  199.1 48.0 %copy-start.17 = (s32[2]{0:T(128)S(1)}, s32[2]{0:T(128)}, u32[]{:S(2)}) copy-start(s32[2]{0:T(128)} %param.3) | copy-start | bytes 28
  241.6 58.1 %all-to-all-start.3 = ((f32[1,4,512,512]{3,0,1,2:T(1,128)}), f32[1,4,512,512]{3,0,1,2:T(1,128)}, u32[]{:S(2)}, u32[]{:S(2)}) async-start(f32[1,4,512,512]{3,0,1,2:T(1,128)} %copy.154), calls=%async_computation.3 | async-start | bytes 8388608 | tf_op jit(solution)/shard_map/all_to_all | solution.py:122
  253.1 2.0 copy-start.3
  299.7 3.4 copy-start.4
  331.2 8.8 %copy-start.8 = (f32[1,1,128,4,512]{4,2,0,3,1:T(8,128)S(1)}, f32[1,1,128,4,512]{4,2,0,3,1:T(8,128)}, u32[]{:S(2)}) copy-start(f32[1,1,128,4,512]{4,2,0,3,1:T(8,128)} %stack.262) | copy-start | bytes 3145732
  333.6 7.5 %copy-start.9 = (f32[1,1,128,4,512]{4,2,0,3,1:T(8,128)S(1)}, f32[1,1,128,4,512]{4,2,0,3,1:T(8,128)}, u32[]{:S(2)}) copy-start(f32[1,1,128,4,512]{4,2,0,3,1:T(8,128)} %stack.263) | copy-start | bytes 3145732
  337.3 4.8 copy-start.10
  340.0 3.2 copy-start.7
  340.0 3.5 copy-start.11
  340.0 3.9 copy-start.12
  341.0 3.3 copy-start.13
  343.5 2.3 copy-start.6
  345.8 1.8 copy-start.15
  347.7 8.9 %copy-start.16 = (f32[4,128,4]{1,2,0:T(4,128)S(1)}, f32[4,128,4]{1,2,0:T(4,128)}, u32[]{:S(2)}) copy-start(f32[4,128,4]{1,2,0:T(4,128)} %broadcast_add_fusion) | copy-start | bytes 24580
  403.1 2.3 copy-start
  411.0 58.1 %all-to-all-start.4 = ((f32[512,4,512]{2,1,0:T(4,128)}), f32[512,4,512]{2,1,0:T(4,128)}, u32[]{:S(2)}, u32[]{:S(2)}) async-start(f32[512,4,512]{2,1,0:T(4,128)} %copy.166), calls=%async_computation.4 | async-start | bytes 8388608 | tf_op jit(solution)/shard_map/all_to_all | solution.py:165
  469.1 58.5 %all-to-all-start.5 = ((f32[512,4,512]{2,1,0:T(4,128)}), f32[512,4,512]{2,1,0:T(4,128)}, u32[]{:S(2)}, u32[]{:S(2)}) async-start(f32[512,4,512]{2,1,0:T(4,128)} %copy.169), calls=%async_computation.5 | async-start | bytes 8388608 | tf_op jit(solution)/shard_map/all_to_all | solution.py:168
  552.0 2.3 copy-start.1
  559.6 54.6 %all-to-all-start.6 = ((f32[4,512,512]{2,0,1:T(4,128)}), f32[4,512,512]{2,0,1:T(4,128)}, u32[]{:S(2)}, u32[]{:S(2)}) async-start(f32[4,512,512]{2,0,1:T(4,128)} %copy.172), calls=%async_computation.6 | async-start | bytes 8388608 | tf_op jit(solution)/shard_map/all_to_all | solution.py:184
  614.2 53.8 %all-to-all-start.7 = ((f32[4,512,512]{2,0,1:T(4,128)}), f32[4,512,512]{2,0,1:T(4,128)}, u32[]{:S(2)}, u32[]{:S(2)}) async-start(f32[4,512,512]{2,0,1:T(4,128)} %copy.175), calls=%async_computation.7 | async-start | bytes 8388608 | tf_op jit(solution)/shard_map/all_to_all | solution.py:185
  679.4 3.4 copy-start.5
where the time goes:
time: 741 us; the launch traced here: 730 us
  waiting for transfers between devices  290 us (39%)
  local copies, waits for them, and re-layouts  201 us (27%)
  other arithmetic  83.4 us (11%)
  blocking collectives  57.4 us (8%)
  matrix products  55.2 us (7%)
  starting transfers between devices  40.6 us (5%)
    all_to_all x1, blocking collectives, per_device(): lax.all_to_all(real_part, 'gy', split_axis=0, concat_axis=1, tiled=True)  57.4 us
    dot_general x6, matrix products, product_section(): jnp.einsum(joined_form, stacked, block_table, precision=HIGHEST, preferre...  55.2 us
    all_to_all x1, waiting for transfers between devices, per_device(): lax.all_to_all(imag_part, 'gy', split_axis=0, concat_axis=1, tiled=True)  44.3 us
    all_to_all x1, waiting for transfers between devices, per_device(): lax.all_to_all(packed_re.reshape(flat_x), ('gx', 'gy'), split_axis=0, con...  44 us
    all_to_all x1, waiting for transfers between devices, per_device(): lax.all_to_all(real_part[None], ('gx', 'gy'), split_axis=2, concat_axis=0...  42.6 us
    all_to_all x1, waiting for transfers between devices, per_device(): lax.all_to_all(imag_part[None], ('gx', 'gy'), split_axis=2, concat_axis=0...  42.3 us
    all_to_all x1, waiting for transfers between devices, per_device(): lax.all_to_all(packed_re.reshape(flat_y), 'gy', split_axis=1, concat_axis...  42.1 us
    all_to_all x1, waiting for transfers between devices, per_device(): lax.all_to_all(packed_im.reshape(flat_x), ('gx', 'gy'), split_axis=0, con...  42 us
  transfers between devices with their start and end apart: 7, of which 7 were waited for; matrix products, arithmetic and copies ran while one was open for 9% of the time, Pallas kernels for 0%

commit v1 on v0

v1 whole, which is shorter than its diff:
```python
import math

import jax
import jax.numpy as jnp
import ml_dtypes
import numpy as np
from jax import lax
from jax.experimental import pallas as pl
from jax.experimental.pallas import tpu as pltpu
from jax.sharding import PartitionSpec as P

N = 512
HALF = 256
QUARTER = 128
GX = 16
GY = 8
AXES = ("gx", "gy")
F32 = jnp.float32
BF16 = jnp.bfloat16
VMEM_LIMIT = 56 * 1024 * 1024


def frequencies():
    m = np.arange(QUARTER)
    even = np.concatenate([2 * m, np.where(m == 0, 256, 2 * m)])
    odd = np.concatenate([2 * m + 1, 2 * m + 1])
    return even, odd


def basis():
    n = np.arange(HALF)
    tables = []
    for freq in frequencies():
        angle = 2.0 * np.pi / N * ((freq[:, None] * n[None, :]) % N)
        is_cos = (np.arange(HALF) < QUARTER) | (freq == 256)
        table = np.where(is_cos[:, None], np.cos(angle), np.sin(angle))
        weight = np.where((freq == 0) | (freq == 256), 1.0, 2.0)
        tables.append(table * np.sqrt(weight / N)[:, None])
    return np.stack(tables)


def two_parts(table):
    high = table.astype(ml_dtypes.bfloat16)
    low = (table - high.astype(np.float64)).astype(ml_dtypes.bfloat16)
    return high, low


def left_table(table):
    high, low = two_parts(table)
    return np.concatenate([high, high, low], axis=2)


def right_table(table):
    high, low = two_parts(table)
    return np.concatenate([high, high, low], axis=1)


def x_order():
    x = np.arange(HALF).reshape(8, 16, 2)
    return x.transpose(2, 0, 1).reshape(-1)


def split(value):
    high = value.astype(BF16)
    low = (value - high.astype(F32)).astype(BF16)
    return high, low


def head_kernel(d_ref, table_ref, o_ref):
    first = d_ref[:, :, :HALF].reshape(1024, HALF)
    second = d_ref[:, :, HALF:].reshape(1024, HALF)
    rows = o_ref.reshape(128 * 4 * 8, 128)
    for parity in range(2):
        high, low = split(first + second if parity == 0 else first - second)
        data = jnp.concatenate([high, low, high], axis=1)
        out = lax.dot_general(
            table_ref[parity], data, (((1,), (1,)), ((), ())), preferred_element_type=F32
        )
        for half in range(2):
            for x in range(8):
                rows[pl.ds((2 * parity + half) * 8 + x, 128, stride=32), :] = out[
                    half * 128 : (half + 1) * 128, x * 128 : (x + 1) * 128
                ]


def middle_kernel(r_ref, w_ref, yf_ref, xf_ref, xi_ref, yi_ref, o_ref, lhs_ref, rhs_ref):
    low_lanes = lax.broadcasted_iota(jnp.int32, (256, 128), 1) < 64

    def merge(a, b):
        return (
            jnp.where(low_lanes, a, pltpu.roll(b, 64, 1)),
            jnp.where(low_lanes, pltpu.roll(a, 64, 1), b),
        )

    def put_lhs(slot, rows, cols, value):
        high, low = split(value)
        lhs_ref[slot, pl.ds(rows, value.shape[0]), pl.ds(cols, value.shape[1])] = high
        lhs_ref[slot, pl.ds(rows, value.shape[0]), pl.ds(cols + HALF, value.shape[1])] = low

    def put_rhs(slot, cols, value):
        high, low = split(value)
        rhs_ref[slot, :HALF, pl.ds(cols, value.shape[1])] = high
        rhs_ref[slot, HALF:, pl.ds(cols, value.shape[1])] = low

    def times_right(slot, table):
        data = jnp.concatenate([lhs_ref[slot], lhs_ref[slot, :, :HALF]], axis=1)
        return jnp.dot(data, table, preferred_element_type=F32)

    def times_left(table, slot):
        data = jnp.concatenate([rhs_ref[slot], rhs_ref[slot, :HALF, :]], axis=0)
        return jnp.dot(table, data, preferred_element_type=F32)

    for pair in range(2):
        low_a = r_ref[:, 2 * pair, 0].reshape(256, 128)
        low_b = r_ref[:, 2 * pair + 1, 0].reshape(256, 128)
        high_a = r_ref[:, 2 * pair + 4, 0].reshape(256, 128)
        high_b = r_ref[:, 2 * pair + 5, 0].reshape(256, 128)
        for parity in range(2):
            a = low_a + high_a if parity == 0 else low_a - high_a
            b = low_b + high_b if parity == 0 else low_b - high_b
            even_x, odd_x = merge(a, b)
            put_lhs(parity, 0, pair * 128, even_x)
            put_lhs(parity, 256, pair * 128, odd_x)
    for parity in range(2):
        out = times_right(parity, yf_ref[parity]).reshape(2, 2, 128, HALF)
        put_rhs(0, parity * HALF, (out[:, 0] + out[:, 1]).reshape(HALF, HALF))
        put_rhs(1, parity * HALF, (out[:, 0] - out[:, 1]).reshape(HALF, HALF))
    for parity in range(2):
        spectrum = times_left(xf_ref[parity], parity)
        for field in range(2):
            weights = w_ref[0, field, parity * HALF : (parity + 1) * HALF, :]
            put_rhs(2 + 2 * field + parity, 0, spectrum * weights)
    for field in range(2):
        even = times_left(xi_ref[0], 2 + 2 * field)
        odd = times_left(xi_ref[1], 3 + 2 * field)
        for near in range(2):
            value = even + odd if near == 0 else even - odd
            for parity in range(2):
                for p in range(2):
                    put_lhs(
                        parity,
                        p * 256 + near * 128,
                        0,
                        value[p * 128 : (p + 1) * 128, parity * HALF : (parity + 1) * HALF],
                    )
        even = times_right(0, yi_ref[0])
        odd = times_right(1, yi_ref[1])
        for near in range(2):
            value = even + odd if near == 0 else even - odd
            for pair in range(2):
                cols = slice(pair * 128, (pair + 1) * 128)
                first, second = merge(value[:256, cols], value[256:, cols])
                o_ref[:, 4 * near + 2 * pair, 0, field] = first.reshape(16, 16, 128)
                o_ref[:, 4 * near + 2 * pair + 1, 0, field] = second.reshape(16, 16, 128)


def tail_kernel(b_ref, table_ref, o_ref):
    rows = b_ref.reshape(128 * 4 * 8, 128)
    for x in range(8):
        parts = []
        for parity in range(2):
            coefs = jnp.concatenate(
                [
                    rows[pl.ds((2 * parity + half) * 8 + x, 128, stride=32), :].T
                    for half in range(2)
                ],
                axis=1,
            )
            high, low = split(coefs)
            data = jnp.concatenate([high, low, high], axis=1)
            parts.append(jnp.dot(data, table_ref[parity], preferred_element_type=F32))
        o_ref[0, 2 * x : 2 * x + 2, :, :HALF] = (parts[0] + parts[1]).reshape(2, 64, HALF)
        o_ref[0, 2 * x : 2 * x + 2, :, HALF:] = (parts[0] - parts[1]).reshape(2, 64, HALF)


def window(u_value):
    is_small = u_value < 0.2
    safe_u = jnp.where(is_small, 1.0, u_value)
    closed_form = 3.0 * (jnp.sin(safe_u) - safe_u * jnp.cos(safe_u)) / (safe_u * safe_u * safe_u)
    series = 1.0 - u_value * u_value / 10.0 + u_value**4 / 280.0
    return jnp.where(is_small, series, closed_form)


def plane_windows(radius_cells):
    d = lax.axis_index(AXES)
    kz = jnp.stack([2 * d, jnp.where(d == 0, 256, 2 * d), 2 * d + 1]).astype(F32)
    freq = np.concatenate(frequencies()).astype(np.float32)
    squares = jnp.asarray(freq * freq)
    k_squared = (
        (kz * kz)[:, None, None] + squares[None, :, None] + squares[None, None, :]
    )
    k_length = 2.0 * math.pi / N * jnp.sqrt(k_squared)
    radius_values = radius_cells.astype(F32)
    return window(k_length[:, None] * radius_values[None, :, None, None])


def whole(shape):
    return pl.BlockSpec(shape, lambda *_: (0,) * len(shape))


def params(dims):
    return pltpu.CompilerParams(
        dimension_semantics=("arbitrary",) * dims, vmem_limit_bytes=VMEM_LIMIT
    )


def per_device(density, radius_cells):
    table = basis()
    back = table.transpose(0, 2, 1)
    x_table = table[:, :, x_order()]
    x_back = x_table.transpose(0, 2, 1)
    coefs = pl.pallas_call(
        head_kernel,
        grid=(2,),
        in_specs=[
            pl.BlockSpec((16, 64, N), lambda i: (i, 0, 0)),
            whole((2, HALF, 3 * HALF)),
        ],
        out_specs=pl.BlockSpec((128, 4, 8, 128), lambda i: (0, 0, i, 0)),
        out_shape=jax.ShapeDtypeStruct((128, 4, 16, 128), F32),
        compiler_params=params(1),
    )(density, jnp.asarray(left_table(table)))
    planes = lax.all_to_all(coefs, AXES, split_axis=0, concat_axis=0, tiled=True)
    weights = plane_windows(radius_cells)
    planes = planes.reshape(GX, GY, 4, 16, 128)
    filtered = pl.pallas_call(
        middle_kernel,
        grid=(4,),
        in_specs=[
            pl.BlockSpec((GX, GY, 1, 16, 128), lambda s: (0, 0, s, 0, 0)),
            pl.BlockSpec((1, 2, N, N), lambda s: (jnp.minimum(s, 2), 0, 0, 0)),
            whole((2, 3 * HALF, HALF)),
            whole((2, HALF, 3 * HALF)),
            whole((2, HALF, 3 * HALF)),
            whole((2, 3 * HALF, HALF)),
        ],
        out_specs=pl.BlockSpec((GX, GY, 1, 2, 16, 128), lambda s: (0, 0, s, 0, 0, 0)),
        out_shape=jax.ShapeDtypeStruct((GX, GY, 4, 2, 16, 128), F32),
        scratch_shapes=[
            pltpu.VMEM((2, N, N), BF16),
            pltpu.VMEM((6, N, N), BF16),
        ],
        compiler_params=params(1),
    )(
        planes,
        weights,
        jnp.asarray(right_table(back)),
        jnp.asarray(left_table(x_table)),
        jnp.asarray(left_table(x_back)),
        jnp.asarray(right_table(table)),
    )
    filtered = filtered.reshape(128, 4, 2, 16, 128)
    filtered = lax.all_to_all(filtered, AXES, split_axis=0, concat_axis=0, tiled=True)
    return pl.pallas_call(
        tail_kernel,
        grid=(2, 2),
        in_specs=[
            pl.BlockSpec((128, 4, 1, 8, 128), lambda f, i: (0, 0, f, i, 0)),
            whole((2, 3 * HALF, HALF)),
        ],
        out_specs=pl.BlockSpec((1, 16, 64, N), lambda f, i: (f, i, 0, 0)),
        out_shape=jax.ShapeDtypeStruct((2, 32, 64, N), F32),
        compiler_params=params(2),
    )(filtered, jnp.asarray(right_table(table)))


def solution(mesh):
    return jax.shard_map(
        per_device,
        mesh=mesh,
        in_specs=(P("gx", "gy", None), P()),
        out_specs=P(None, "gx", "gy", None),
        check_vma=False,
    )
```

time: 741 us -> 207 us (0.28); the launches traced: 730 us -> 206 us
  waiting for transfers between devices: 290 us -> 24.4 us
  local copies, waits for them, and re-layouts: 201 us -> 0.01 us
  other arithmetic: 83.4 us -> 27.9 us
  matrix products: 55.2 us -> 0 us
  blocking collectives: 57.4 us -> 104 us
  Pallas kernels: 0 us -> 38.1 us
  starting transfers between devices: 40.6 us -> 12 us
    all_to_all x7 -> x1, waiting for transfers between devices: 290 us -> 24.4 us  [per_device(): lax.all_to_all(coefs, AXES, split_axis=0, concat_axis=0, tiled=True)]
    another operation x21 -> x0, local copies, waits for them, and re-layouts: 68.6 us -> none  [the longest x6 29.1 us: product_section(): stacked = jnp.stack([real_part, imag_part], 0)]
    dot_general x6 -> x0, matrix products: 55.2 us -> none  [product_section(): jnp.einsum(joined_form, stacked, block_table, precision=HIGHEST, preferre...]
    sub x9 -> x0, other arithmetic: 49.4 us -> none  [the longest x1 36.2 us: per_device(): packed_re = real_part * weight_first - imag_part * weight_second]
    all_to_all x1, blocking collectives: 57.4 us -> 104 us  [per_device(): lax.all_to_all(filtered, AXES, split_axis=0, concat_axis=0, tiled=True)]
    pallas_call x0 -> x3, Pallas kernels: none -> 38.1 us  [the longest x1 19 us: per_device(): pl.pallas_call(middle_kernel, grid=(4,), in_specs=[pl.BlockSpec((GX, GY,...]
    all_to_all x8 -> x0, local copies, waits for them, and re-layouts: 29.8 us -> none  [the longest x2 6.13 us: per_device(): lax.all_to_all(packed_re.reshape(flat_y), 'gy', split_axis=1, concat_axis...]
    all_to_all x7 -> x1, starting transfers between devices: 40.6 us -> 12 us  [per_device(): lax.all_to_all(coefs, AXES, split_axis=0, concat_axis=0, tiled=True)]
  transfers between devices with their start and end apart: 7 -> 1, of which waited for: 7 -> 1; matrix products, arithmetic and copies ran while one was open for 9% -> 14% of each run, Pallas kernels for 0% -> 0%
where the time goes in v1:
time: 207 us; the launch traced here: 206 us
  blocking collectives  104 us (50%)
  Pallas kernels  38.1 us (18%)
  other arithmetic  27.9 us (13%)
  waiting for transfers between devices  24.4 us (12%)
  starting transfers between devices  12 us (6%)
    all_to_all x1, blocking collectives, per_device(): lax.all_to_all(filtered, AXES, split_axis=0, concat_axis=0, tiled=True)  104 us
    select_n x1, other arithmetic, window(): return jnp.where(is_small, series, closed_form)  26.8 us
    all_to_all x1, waiting for transfers between devices, per_device(): lax.all_to_all(coefs, AXES, split_axis=0, concat_axis=0, tiled=True)  24.4 us
    pallas_call x1, Pallas kernels, per_device(): pl.pallas_call(middle_kernel, grid=(4,), in_specs=[pl.BlockSpec((GX, GY,...  19 us
    pallas_call x1, Pallas kernels, per_device(): pl.pallas_call(tail_kernel, grid=(2, 2), in_specs=[pl.BlockSpec((128, 4,...  12 us
    all_to_all x1, starting transfers between devices, per_device(): lax.all_to_all(coefs, AXES, split_axis=0, concat_axis=0, tiled=True)  12 us
    pallas_call x1, Pallas kernels, per_device(): pl.pallas_call(head_kernel, grid=(2,), in_specs=[pl.BlockSpec((16, 64, N)...  7.16 us
  transfers between devices with their start and end apart: 1, of which 1 were waited for; matrix products, arithmetic and copies ran while one was open for 14% of the time, Pallas kernels for 0%

profile of v1, /device:TPU:1, one launch (start us, length us, event | category | flops | bytes accessed | tf_op | source)
XLA Modules:
  0.0 206.2 jit_solution(16189767591265029160)
XLA Ops:
  0.0 7.2 %shard_map.91 = f32[128,4,16,128]{3,2,1,0:T(8,128)} custom-call(f32[32,64,512]{2,1,0:T(8,128)} %d_ref.1, bf16[2,256,768]{2,1,0:T(8,128)(2,1)} %constant.46.clone.table_ref), custom_call_target="tpu_custom_call" | custom-call | tf_op jit(solution)/shard_map/pallas_call | solution.py:212
  7.2 0.0 copy-start.1
  7.2 0.0 copy-start
  7.2 12.0 %all-to-all-start = ((f32[128,4,16,128]{3,2,1,0:T(8,128)}), f32[128,4,16,128]{3,2,1,0:T(8,128)}, u32[]{:S(2)}, u32[]{:S(2)}) async-start(f32[128,4,16,128]{3,2,1,0:T(8,128)} %shard_map.91), calls=%async_computation | async-start | bytes 8388608 | tf_op jit(solution)/shard_map/all_to_all | solution.py:223
  19.1 0.0 copy-done.1
  19.2 0.1 fusion.14
  19.2 0.0 copy-done
  19.3 0.1 broadcast_add_fusion
  19.3 1.0 sqrt_multiply_fusion
  20.3 26.8 %fusion.7.w_ref = f32[3,2,512,512]{3,2,1,0:T(8,128)} fusion(f32[2]{0:T(128)S(1)} %convert_element_type.11, f32[3,512,512]{2,1,0:T(8,128)S(1)} %sqrt_multiply_fusion), kind=kLoop, calls=%fused_computation.10 | loop fusion | flops 25165824 | bytes 9437192 | tf_op jit(solution)/shard_map/jit(_where)/select_n | solution.py:181
  47.1 24.4 %all-to-all-done = f32[128,4,16,128]{3,2,1,0:T(8,128)} async-done(((f32[128,4,16,128]{3,2,1,0:T(8,128)}), f32[128,4,16,128]{3,2,1,0:T(8,128)}, u32[]{:S(2)}, u32[]{:S(2)}) %all-to-all-start) | async-done | bytes 4194336 | tf_op jit(solution)/shard_map/all_to_all | solution.py:223
  71.6 19.0 %shard_map.92 = f32[16,8,4,2,16,128]{5,4,3,2,1,0:T(8,128)} custom-call(f32[16,8,4,16,128]{4,3,2,1,0:T(8,128)} %bitcast.r_ref, f32[3,2,512,512]{3,2,1,0:T(8,128)} %fusion.7.w_ref, bf16[2,768,256]{2,1,0:T(8,128)(2,1)} %constant.48.clone.yf_ref, bf16[2,256,768]{2,1,0:T(8,128)(2,1)} %constant.49.clone.xf_ref, bf16[2,256,768]{2,1,0:T(8,128)(2,1)} %constant.50.clone.xi_ref, ...), custom_call_target="tpu_custom_call" | custom-call | tf_op jit(solution)/shard_map/pallas_call | solution.py:226
  90.5 103.7 %all_to_all.10.b_ref = f32[128,4,2,16,128]{4,3,2,1,0:T(8,128)} all-to-all(f32[128,4,2,16,128]{4,3,2,1,0:T(8,128)} %bitcast.5), channel_id=1, replica_groups=mesh['gx'=16,'gy'=8] {'gx','gy'}, dimensions={0} | all-to-all | bytes 16777216 | tf_op jit(solution)/shard_map/all_to_all | solution.py:253
  194.2 12.0 %shard_map.93 = f32[2,32,64,512]{3,2,1,0:T(8,128)} custom-call(f32[128,4,2,16,128]{4,3,2,1,0:T(8,128)} %all_to_all.10.b_ref, bf16[2,768,256]{2,1,0:T(8,128)(2,1)} %constant.51.clone.yi_ref.table_ref), custom_call_target="tpu_custom_call" | custom-call | tf_op jit(solution)/shard_map/pallas_call | solution.py:254
  (1 shorter events, 0.0 us)
Async XLA Ops:
  7.2 12.0 %copy-start.1 = (s32[2]{0:T(128)S(1)}, s32[2]{0:T(128)}, u32[]{:S(2)}) copy-start(s32[2]{0:T(128)} %param.10) | copy-start | bytes 28
  7.2 12.1 %copy-start = (f32[512]{0:T(512)S(1)}, f32[512]{0:T(512)}, u32[]{:S(2)}) copy-start(f32[512]{0:T(512)} %constant.47.clone) | copy-start | bytes 6148
  7.2 64.4 %all-to-all-start = ((f32[128,4,16,128]{3,2,1,0:T(8,128)}), f32[128,4,16,128]{3,2,1,0:T(8,128)}, u32[]{:S(2)}, u32[]{:S(2)}) async-start(f32[128,4,16,128]{3,2,1,0:T(8,128)} %shard_map.91), calls=%async_computation | async-start | bytes 8388608 | tf_op jit(solution)/shard_map/all_to_all | solution.py:223

commit v2 on v1

v2 whole, which is shorter than its diff:
```python
import math

import jax
import jax.numpy as jnp
import ml_dtypes
import numpy as np
from jax import lax
from jax.experimental import pallas as pl
from jax.experimental.pallas import tpu as pltpu
from jax.sharding import PartitionSpec as P

N = 512
HALF = 256
QUARTER = 128
GX = 16
GY = 8
AXES = ("gx", "gy")
F32 = jnp.float32
BF16 = jnp.bfloat16
MIB = 1024 * 1024


def frequencies():
    m = np.arange(QUARTER)
    even = np.concatenate([2 * m, np.where(m == 0, HALF, 2 * m)])
    odd = np.concatenate([2 * m + 1, 2 * m + 1])
    return even, odd


def basis():
    n = np.arange(HALF)
    tables = []
    for freq in frequencies():
        angle = 2.0 * np.pi / N * ((freq[:, None] * n[None, :]) % N)
        is_cos = (np.arange(HALF) < QUARTER) | (freq == HALF)
        table = np.where(is_cos[:, None], np.cos(angle), np.sin(angle))
        weight = np.where((freq == 0) | (freq == HALF), 1.0, 2.0)
        tables.append(table * np.sqrt(weight / N)[:, None])
    return np.stack(tables)


def two_parts(table):
    high = table.astype(ml_dtypes.bfloat16)
    low = (table - high.astype(np.float64)).astype(ml_dtypes.bfloat16)
    return jnp.asarray(np.concatenate([high, low], axis=2))


def split(value):
    high = value.astype(BF16)
    low = (value - high.astype(F32)).astype(BF16)
    return high, low


def join(high, low, axis):
    return jnp.concatenate([high, low, high], axis=axis)


def join_table(table, axis):
    high, low = table[:, :HALF], table[:, HALF:]
    return jnp.concatenate([high, high, low], axis=axis)


def head_kernel(d_ref, table_ref, o_ref):
    def rows(cols):
        return jnp.concatenate([d_ref[p, x, :, cols] for x in range(8) for p in range(2)], axis=0)

    first, second = rows(slice(0, HALF)), rows(slice(HALF, N))
    for parity in range(2):
        data = join(*split(first + second if parity == 0 else first - second), 1)
        out = lax.dot_general(
            join_table(table_ref[parity], 1),
            data,
            (((1,), (1,)), ((), ())),
            preferred_element_type=F32,
        )
        for half in range(2):
            part = out[half * 128 : (half + 1) * 128]
            chunks = jnp.stack([part[:, x * 128 : (x + 1) * 128] for x in range(8)])
            o_ref[:, 2 * parity + half] = jnp.swapaxes(chunks, 0, 1)


def middle_kernel(r_ref, w_ref, table_ref, back_ref, o_ref, lhs_ref, rhs_ref):
    low_lanes = lax.broadcasted_iota(jnp.int32, (16, 16, 128), 2) < 64

    def merge(a, b):
        return (
            jnp.where(low_lanes, a, pltpu.roll(b, 64, 2)),
            jnp.where(low_lanes, pltpu.roll(a, 64, 2), b),
        )

    def put_rhs(slot, value):
        high, low = split(value)
        rhs_ref[slot, :HALF, :] = high
        rhs_ref[slot, HALF:, :] = low

    def times_right(slot, table):
        data = lhs_ref[slot].reshape(N, N)
        data = join(data[:, :HALF], data[:, HALF:], 1)
        return jnp.dot(data, join_table(table, 0), preferred_element_type=F32)

    def times_left(table, slot):
        data = join(rhs_ref[slot, :HALF, :], rhs_ref[slot, HALF:, :], 0)
        return jnp.dot(join_table(table, 1), data, preferred_element_type=F32)

    def load(parity):
        for pair in range(2):
            low_a, low_b = r_ref[:, 2 * pair, 0], r_ref[:, 2 * pair + 1, 0]
            high_a, high_b = r_ref[:, 2 * pair + 4, 0], r_ref[:, 2 * pair + 5, 0]
            a = low_a + high_a if parity == 0 else low_a - high_a
            b = low_b + high_b if parity == 0 else low_b - high_b
            for p, value in enumerate(merge(a, b)):
                high, low = split(value)
                cols = slice(pair * 128, (pair + 1) * 128)
                lhs_ref[parity, :, p, :, cols] = high
                cols = slice(HALF + pair * 128, HALF + (pair + 1) * 128)
                lhs_ref[parity, :, p, :, cols] = low

    def forward_y(parity):
        return times_right(parity, back_ref[parity])

    def after_y(parity, out):
        put_rhs(2 * parity, out[:HALF] + out[HALF:])
        put_rhs(2 * parity + 1, out[:HALF] - out[HALF:])

    def forward_x(parity, x_parity):
        return times_left(table_ref[x_parity], 2 * parity + x_parity)

    def window_block(field, x_parity, parity):
        rows = slice(x_parity * 128, (x_parity + 1) * 128)
        if parity == 0:
            upper = w_ref[0, field, rows, :HALF]
        else:
            odd = w_ref[0, field, rows, HALF:]
            upper = jnp.concatenate([odd, odd], axis=1)
        if x_parity == 1:
            return jnp.concatenate([upper, upper], axis=0)
        last = w_ref[0, field, HALF:, :HALF]
        if parity == 1:
            last = w_ref[0, field, HALF:, HALF:]
            last = jnp.concatenate([last, last], axis=1)
        is_first = lax.broadcasted_iota(jnp.int32, (8, HALF), 0) == 0
        return jnp.concatenate([upper, jnp.where(is_first, last, upper[:8]), upper[8:]], axis=0)

    def after_x(parity, x_parity, out):
        for field in range(2):
            weights = window_block(field, x_parity, parity)
            put_rhs(4 + 4 * field + 2 * parity + x_parity, out * weights)

    def inverse_x(field, parity):
        slot = 4 + 4 * field + 2 * parity
        return times_left(back_ref[0], slot), times_left(back_ref[1], slot + 1)

    def after_inverse_x(field, parity, out):
        for near in range(2):
            value = out[0] + out[1] if near == 0 else out[0] - out[1]
            high, low = split(value)
            gx = slice(near * 8, (near + 1) * 8)
            lhs_ref[2 + 2 * field + parity, gx, :, :, :HALF] = high.reshape(8, 2, 16, HALF)
            lhs_ref[2 + 2 * field + parity, gx, :, :, HALF:] = low.reshape(8, 2, 16, HALF)

    def inverse_y(field, parity):
        return times_right(2 + 2 * field + parity, table_ref[parity])

    def finish(field, even, odd):
        for near in range(2):
            value = even + odd if near == 0 else even - odd
            value = value.reshape(16, 2, 16, HALF)
            for pair in range(2):
                cols = slice(pair * 128, (pair + 1) * 128)
                first, second = merge(value[:, 0, :, cols], value[:, 1, :, cols])
                o_ref[:, 4 * near + 2 * pair, 0, field] = first
                o_ref[:, 4 * near + 2 * pair + 1, 0, field] = second

    load(0)
    y0 = forward_y(0)
    load(1)
    y1 = forward_y(1)
    after_y(0, y0)
    x00 = forward_x(0, 0)
    x01 = forward_x(0, 1)
    after_y(1, y1)
    x10 = forward_x(1, 0)
    after_x(0, 0, x00)
    after_x(0, 1, x01)
    x11 = forward_x(1, 1)
    i00 = inverse_x(0, 0)
    after_x(1, 0, x10)
    after_x(1, 1, x11)
    i01 = inverse_x(0, 1)
    after_inverse_x(0, 0, i00)
    i10 = inverse_x(1, 0)
    after_inverse_x(0, 1, i01)
    f0 = inverse_y(0, 0)
    after_inverse_x(1, 0, i10)
    g0 = inverse_y(0, 1)
    i11 = inverse_x(1, 1)
    finish(0, f0, g0)
    f1 = inverse_y(1, 0)
    after_inverse_x(1, 1, i11)
    finish(1, f1, inverse_y(1, 1))


def tail_kernel(b_ref, table_ref, o_ref, lhs_ref):
    def load(parity):
        for half in range(2):
            chunks = jnp.swapaxes(b_ref[:, 2 * parity + half, 0], 0, 1)
            for x in range(8):
                rows = slice(x * 128, (x + 1) * 128)
                for part, value in enumerate(split(chunks[x])):
                    start = part * HALF + half * 128
                    lhs_ref[parity, rows, start : start + 128] = value.T

    def transform(parity):
        data = join(lhs_ref[parity, :, :HALF], lhs_ref[parity, :, HALF:], 1)
        return jnp.dot(data, join_table(table_ref[parity], 0), preferred_element_type=F32)

    def store(cols, value):
        value = value.reshape(8, 2, 64, HALF)
        for p in range(2):
            o_ref[0, p, :, :, cols] = value[:, p]

    load(0)
    even = transform(0)
    load(1)
    odd = transform(1)
    store(slice(0, HALF), even + odd)
    store(slice(HALF, N), even - odd)


def window(u_value):
    is_small = u_value < 0.2
    safe_u = jnp.where(is_small, 1.0, u_value)
    closed_form = 3.0 * (jnp.sin(safe_u) - safe_u * jnp.cos(safe_u)) / (safe_u * safe_u * safe_u)
    series = 1.0 - u_value * u_value / 10.0 + u_value**4 / 280.0
    return jnp.where(is_small, series, closed_form)


def plane_windows(radius_cells):
    d = lax.axis_index(AXES)
    kz = jnp.stack([2 * d, jnp.where(d == 0, HALF, 2 * d), 2 * d + 1]).astype(F32)
    even, odd = frequencies()
    rows = np.concatenate([even[:QUARTER], odd[:QUARTER], np.full(8, HALF)])
    cols = np.concatenate([even, odd[:QUARTER]])
    row_squares = jnp.asarray((rows * rows).astype(np.float32))
    col_squares = jnp.asarray((cols * cols).astype(np.float32))
    k_squared = (
        (kz * kz)[:, None, None] + row_squares[None, :, None] + col_squares[None, None, :]
    )
    k_length = 2.0 * math.pi / N * jnp.sqrt(k_squared)
    radius_values = radius_cells.astype(F32)
    return window(k_length[:, None] * radius_values[None, :, None, None])


def whole(shape):
    return pl.BlockSpec(shape, lambda *_: (0,) * len(shape))


TABLE = (2, HALF, N)


def z_forward(density, table):
    return pl.pallas_call(
        head_kernel,
        grid=(2,),
        in_specs=[pl.BlockSpec((2, 8, 64, N), lambda i: (0, i, 0, 0)), whole(TABLE)],
        out_specs=pl.BlockSpec((128, 4, 8, 128), lambda i: (0, 0, i, 0)),
        out_shape=jax.ShapeDtypeStruct((128, 4, 16, 128), F32),
        compiler_params=pltpu.CompilerParams(vmem_limit_bytes=56 * MIB),
    )(density.reshape(2, 16, 64, N), table)


def filter_planes(planes, weights, table, back):
    return pl.pallas_call(
        middle_kernel,
        grid=(4,),
        in_specs=[
            pl.BlockSpec((GX, GY, 1, 16, 128), lambda s: (0, 0, s, 0, 0)),
            pl.BlockSpec((1, 2, HALF + 8, HALF + QUARTER), lambda s: (jnp.minimum(s, 2), 0, 0, 0)),
            whole(TABLE),
            whole(TABLE),
        ],
        out_specs=pl.BlockSpec((GX, GY, 1, 2, 16, 128), lambda s: (0, 0, s, 0, 0, 0)),
        out_shape=jax.ShapeDtypeStruct((GX, GY, 4, 2, 16, 128), F32),
        scratch_shapes=[
            pltpu.VMEM((6, GX, 2, 16, N), BF16),
            pltpu.VMEM((12, N, HALF), BF16),
        ],
        compiler_params=pltpu.CompilerParams(vmem_limit_bytes=28 * MIB),
    )(planes, weights, table, back)


def z_inverse(filtered, table):
    out = pl.pallas_call(
        tail_kernel,
        grid=(2, 2),
        in_specs=[pl.BlockSpec((128, 4, 1, 8, 128), lambda f, i: (0, 0, f, i, 0)), whole(TABLE)],
        out_specs=pl.BlockSpec((1, 2, 8, 64, N), lambda f, i: (f, 0, i, 0, 0)),
        out_shape=jax.ShapeDtypeStruct((2, 2, 16, 64, N), F32),
        scratch_shapes=[pltpu.VMEM((2, 1024, N), BF16)],
        compiler_params=pltpu.CompilerParams(vmem_limit_bytes=28 * MIB),
    )(filtered, table)
    return out.reshape(2, 32, 64, N)


def exchange(pieces):
    return lax.all_to_all(pieces, AXES, split_axis=0, concat_axis=0, tiled=True)


def per_device(density, radius_cells):
    table = two_parts(basis())
    back = two_parts(basis().transpose(0, 2, 1))
    planes = exchange(z_forward(density, table))
    weights = plane_windows(radius_cells)
    filtered = filter_planes(planes.reshape(GX, GY, 4, 16, 128), weights, table, back)
    return z_inverse(exchange(filtered.reshape(128, 4, 2, 16, 128)), table)


def solution(mesh):
    return jax.shard_map(
        per_device,
        mesh=mesh,
        in_specs=(P("gx", "gy", None), P()),
        out_specs=P(None, "gx", "gy", None),
        check_vma=False,
    )
```

time: 207 us -> 196 us (0.947)
  waiting for transfers between devices: 24.4 us -> 42.1 us
  other arithmetic: 27.9 us -> 10.3 us
  Pallas kernels: 38.1 us -> 29 us
    all_to_all x1, waiting for transfers between devices: 24.4 us -> 42.1 us  [exchange(): return lax.all_to_all(pieces, AXES, split_axis=0, concat_axis=0, tiled=True)]
    select_n x1, other arithmetic: 26.8 us -> 9.71 us  [window(): return jnp.where(is_small, series, closed_form)]
    pallas_call x3, Pallas kernels: 38.1 us -> 29 us  [the longest x1 14.9 us: filter_planes(): pl.pallas_call(middle_kernel, grid=(4,), in_specs=[pl.BlockSpec((GX, GY,...]
  transfers between devices with their start and end apart: 1 -> 1, of which waited for: 1 -> 1; matrix products, arithmetic and copies ran while one was open for 14% -> 5% of each run, Pallas kernels for 0% -> 0%
where the time goes in v2:
time: 196 us
  blocking collectives  103 us (53%)
  waiting for transfers between devices  42.1 us (21%)
  Pallas kernels  29 us (15%)
  starting transfers between devices  12 us (6%)
  other arithmetic  10.3 us (5%)
    all_to_all x1, blocking collectives, exchange(): return lax.all_to_all(pieces, AXES, split_axis=0, concat_axis=0, tiled=True)  103 us
    all_to_all x1, waiting for transfers between devices, exchange(): return lax.all_to_all(pieces, AXES, split_axis=0, concat_axis=0, tiled=True)  42.1 us
    pallas_call x1, Pallas kernels, filter_planes(): pl.pallas_call(middle_kernel, grid=(4,), in_specs=[pl.BlockSpec((GX, GY,...  14.9 us
    all_to_all x1, starting transfers between devices, exchange(): return lax.all_to_all(pieces, AXES, split_axis=0, concat_axis=0, tiled=True)  12 us
    select_n x1, other arithmetic, window(): return jnp.where(is_small, series, closed_form)  9.71 us
    pallas_call x1, Pallas kernels, z_inverse(): pl.pallas_call(tail_kernel, grid=(2, 2), in_specs=[pl.BlockSpec((128, 4,...  8.51 us
    pallas_call x1, Pallas kernels, z_forward(): pl.pallas_call(head_kernel, grid=(2,), in_specs=[pl.BlockSpec((2, 8, 64,...  5.61 us
  transfers between devices with their start and end apart: 1, of which 1 were waited for; matrix products, arithmetic and copies ran while one was open for 5% of the time, Pallas kernels for 0%

profile of v2, /device:TPU:1, one launch (start us, length us, event | category | flops | bytes accessed | tf_op | source)
XLA Modules:
  0.0 196.0 jit_solution(18394940161994189214)
XLA Ops:
  0.0 5.6 %shard_map.64 = f32[128,4,16,128]{3,2,1,0:T(8,128)} custom-call(f32[2,16,64,512]{3,2,1,0:T(8,128)} %bitcast.8, bf16[2,256,512]{2,1,0:T(8,128)(2,1)} %constant.42.clone.table_ref), custom_call_target="tpu_custom_call" | custom-call | tf_op jit(solution)/shard_map/pallas_call | solution.py:262
  5.6 0.0 copy-start.4
  5.6 0.0 copy-start.3
  5.6 0.0 copy-start.2
  5.6 12.0 %all-to-all-start = ((f32[128,4,16,128]{3,2,1,0:T(8,128)}), f32[128,4,16,128]{3,2,1,0:T(8,128)}, u32[]{:S(2)}, u32[]{:S(2)}) async-start(f32[128,4,16,128]{3,2,1,0:T(8,128)} %shard_map.64), calls=%async_computation | async-start | bytes 8388608 | tf_op jit(solution)/shard_map/all_to_all | solution.py:306
  17.6 0.0 copy-done.4
  17.6 0.1 fusion.14
  17.7 0.0 copy-done.3
  17.7 0.1 broadcast_add_fusion
  17.8 0.0 copy-done.2
  17.8 0.0 copy-start
  17.8 0.0 copy-start.1
  17.8 0.4 sqrt_multiply_fusion
  18.2 9.7 %fusion.7.w_ref = f32[3,2,264,384]{3,2,1,0:T(8,128)S(1)} fusion(f32[2]{0:T(128)S(1)} %convert_element_type.11, f32[3,264,384]{2,1,0:T(8,128)S(1)} %sqrt_multiply_fusion), kind=kLoop, calls=%fused_computation.10 | loop fusion | flops 9732096 | bytes 3649544 | tf_op jit(solution)/shard_map/jit(_where)/select_n | solution.py:235
  27.9 42.1 %all-to-all-done = f32[128,4,16,128]{3,2,1,0:T(8,128)} async-done(((f32[128,4,16,128]{3,2,1,0:T(8,128)}), f32[128,4,16,128]{3,2,1,0:T(8,128)}, u32[]{:S(2)}, u32[]{:S(2)}) %all-to-all-start) | async-done | bytes 4194336 | tf_op jit(solution)/shard_map/all_to_all | solution.py:306
  70.0 0.0 copy-done
  70.0 0.0 copy-done.1
  70.0 14.9 %shard_map.65 = f32[16,8,4,2,16,128]{5,4,3,2,1,0:T(8,128)S(1)} custom-call(f32[16,8,4,16,128]{4,3,2,1,0:T(8,128)} %bitcast.1.r_ref, f32[3,2,264,384]{3,2,1,0:T(8,128)S(1)} %fusion.7.w_ref, bf16[2,256,512]{2,1,0:T(8,128)(2,1)S(1)} %copy-done, bf16[2,256,512]{2,1,0:T(8,128)(2,1)S(1)} %copy-done.1), custom_call_target="tpu_custom_call" | custom-call | tf_op jit(solution)/shard_map/pallas_call | solution.py:273
  84.9 102.6 %all_to_all.10.b_ref = f32[128,4,2,16,128]{4,3,2,1,0:T(8,128)S(1)} all-to-all(f32[128,4,2,16,128]{4,3,2,1,0:T(8,128)S(1)} %bitcast.7), channel_id=1, replica_groups=mesh['gx'=16,'gy'=8] {'gx','gy'}, dimensions={0} | all-to-all | bytes 16777216 | tf_op jit(solution)/shard_map/all_to_all | solution.py:306
  187.5 8.5 %shard_map.66 = f32[2,2,16,64,512]{4,3,2,1,0:T(8,128)} custom-call(f32[128,4,2,16,128]{4,3,2,1,0:T(8,128)S(1)} %all_to_all.10.b_ref, bf16[2,256,512]{2,1,0:T(8,128)(2,1)S(1)} %copy-done), custom_call_target="tpu_custom_call" | custom-call | tf_op jit(solution)/shard_map/pallas_call | solution.py:293
  (1 shorter events, 0.0 us)
Async XLA Ops:
  5.6 12.0 %copy-start.4 = (s32[2]{0:T(128)S(1)}, s32[2]{0:T(128)}, u32[]{:S(2)}) copy-start(s32[2]{0:T(128)} %param.7) | copy-start | bytes 28
  5.6 12.1 %copy-start.3 = (f32[264]{0:T(512)S(1)}, f32[264]{0:T(512)}, u32[]{:S(2)}) copy-start(f32[264]{0:T(512)} %constant.44.clone) | copy-start | bytes 3172
  5.6 12.2 %copy-start.2 = (f32[384]{0:T(512)S(1)}, f32[384]{0:T(512)}, u32[]{:S(2)}) copy-start(f32[384]{0:T(512)} %constant.45.clone) | copy-start | bytes 4612
  5.6 64.4 %all-to-all-start = ((f32[128,4,16,128]{3,2,1,0:T(8,128)}), f32[128,4,16,128]{3,2,1,0:T(8,128)}, u32[]{:S(2)}, u32[]{:S(2)}) async-start(f32[128,4,16,128]{3,2,1,0:T(8,128)} %shard_map.64), calls=%async_computation | async-start | bytes 8388608 | tf_op jit(solution)/shard_map/all_to_all | solution.py:306
  17.8 52.2 %copy-start = (bf16[2,256,512]{2,1,0:T(8,128)(2,1)S(1)}, bf16[2,256,512]{2,1,0:T(8,128)(2,1)}, u32[]{:S(2)}) copy-start(bf16[2,256,512]{2,1,0:T(8,128)(2,1)} %constant.42.clone.table_ref) | copy-start | bytes 1572868
  17.8 52.2 %copy-start.1 = (bf16[2,256,512]{2,1,0:T(8,128)(2,1)S(1)}, bf16[2,256,512]{2,1,0:T(8,128)(2,1)}, u32[]{:S(2)}) copy-start(bf16[2,256,512]{2,1,0:T(8,128)(2,1)} %constant.43.clone.back_ref) | copy-start | bytes 1572868

commit v3 on v2

v3 whole, which is shorter than its diff:
```python
import math

import jax
import jax.numpy as jnp
import ml_dtypes
import numpy as np
from jax import lax
from jax.experimental import pallas as pl
from jax.experimental.pallas import tpu as pltpu
from jax.sharding import PartitionSpec as P

N = 512
HALF = 256
QUARTER = 128
GX = 16
GY = 8
AXES = ("gx", "gy")
F32 = jnp.float32
BF16 = jnp.bfloat16
MIB = 1024 * 1024
CHUNK = 128


def frequencies():
    m = np.arange(QUARTER)
    even = np.concatenate([2 * m, np.where(m == 0, HALF, 2 * m)])
    odd = np.concatenate([2 * m + 1, 2 * m + 1])
    return even, odd


def basis():
    n = np.arange(HALF)
    tables = []
    for freq in frequencies():
        angle = 2.0 * np.pi / N * ((freq[:, None] * n[None, :]) % N)
        is_cos = (np.arange(HALF) < QUARTER) | (freq == HALF)
        table = np.where(is_cos[:, None], np.cos(angle), np.sin(angle))
        weight = np.where((freq == 0) | (freq == HALF), 1.0, 2.0)
        tables.append(table * np.sqrt(weight / N)[:, None])
    return np.stack(tables)


def two_parts(table):
    high = table.astype(ml_dtypes.bfloat16)
    low = (table - high.astype(np.float64)).astype(ml_dtypes.bfloat16)
    return jnp.asarray(np.concatenate([high, low], axis=2))


def split(value):
    high = value.astype(BF16)
    low = (value - high.astype(F32)).astype(BF16)
    return high, low


def join(high, low, axis):
    return jnp.concatenate([high, low, high], axis=axis)


def join_table(table, axis):
    high, low = table[:, :HALF], table[:, HALF:]
    return jnp.concatenate([high, high, low], axis=axis)


def head_kernel(d_ref, table_ref, o_ref):
    def rows(cols):
        return jnp.concatenate([d_ref[p, x, :, cols] for x in range(8) for p in range(2)], axis=0)

    first, second = rows(slice(0, HALF)), rows(slice(HALF, N))
    across = (((1,), (1,)), ((), ()))
    for parity in range(2):
        high, low = split(first + second if parity == 0 else first - second)
        table = jnp.concatenate([table_ref[parity, :, :HALF], table_ref[parity, :, HALF:]], axis=0)
        both = lax.dot_general(table, high, across, preferred_element_type=F32)
        out = both[:HALF] + both[HALF:]
        out += lax.dot_general(table[:HALF], low, across, preferred_element_type=F32)
        for half in range(2):
            part = out[half * 128 : (half + 1) * 128]
            chunks = jnp.stack([part[:, x * 128 : (x + 1) * 128] for x in range(8)])
            o_ref[:, 2 * parity + half] = jnp.swapaxes(chunks, 0, 1)


def middle_kernel(r_ref, w_ref, table_ref, back_ref, o_ref, *scratch):
    lhs_refs, rhs_refs = scratch[:6], scratch[6:]
    def merge(a, b):
        low_lanes = lax.broadcasted_iota(jnp.int32, a.shape, 2) < 64
        return (
            jnp.where(low_lanes, a, pltpu.roll(b, 64, 2)),
            jnp.where(low_lanes, pltpu.roll(a, 64, 2), b),
        )

    def put_rhs(slot, rows, value):
        high, low = split(value)
        rhs_refs[slot][rows, :] = high
        rhs_refs[slot][slice(rows.start + HALF, rows.stop + HALF), :] = low

    def times_right(slot, part, table):
        gx = slice(part * CHUNK // 32, (part + 1) * CHUNK // 32)
        data = lhs_refs[slot][gx].reshape(CHUNK, N)
        data = join(data[:, :HALF], data[:, HALF:], 1)
        return jnp.dot(data, join_table(table, 0), preferred_element_type=F32)

    def times_left(table, slot, part):
        rows = slice(part * CHUNK, (part + 1) * CHUNK)
        data = join(rhs_refs[slot][:HALF, :], rhs_refs[slot][HALF:, :], 0)
        return jnp.dot(join_table(table[rows], 1), data, preferred_element_type=F32)

    def load(parity, pair, half):
        gx = slice(half * 8, half * 8 + 8)
        low_a, low_b = r_ref[gx, 2 * pair, 0], r_ref[gx, 2 * pair + 1, 0]
        high_a, high_b = r_ref[gx, 2 * pair + 4, 0], r_ref[gx, 2 * pair + 5, 0]
        a = low_a + high_a if parity == 0 else low_a - high_a
        b = low_b + high_b if parity == 0 else low_b - high_b
        for p, value in enumerate(merge(a, b)):
            high, low = split(value)
            cols = slice(pair * 128, (pair + 1) * 128)
            lhs_refs[parity][gx, p, :, cols] = high
            cols = slice(HALF + pair * 128, HALF + (pair + 1) * 128)
            lhs_refs[parity][gx, p, :, cols] = low

    parts = HALF // CHUNK

    def forward_y(parity, part):
        table = back_ref[parity]
        return times_right(parity, part, table), times_right(parity, part + parts, table)

    def after_y(parity, part, out):
        rows = slice(part * CHUNK, (part + 1) * CHUNK)
        put_rhs(2 * parity, rows, out[0] + out[1])
        put_rhs(2 * parity + 1, rows, out[0] - out[1])

    def forward_x(parity, x_parity, part):
        return times_left(table_ref[x_parity], 2 * parity + x_parity, part)

    def window_block(field, x_parity, parity, part):
        begin = x_parity * 128 + part * CHUNK % 128
        rows = slice(begin, begin + CHUNK)

        def wide(rows):
            if parity == 0:
                return w_ref[0, field, rows, :HALF]
            odd = w_ref[0, field, rows, HALF:]
            return jnp.concatenate([odd, odd], axis=1)

        weights = wide(rows)
        if x_parity == 1 or part * CHUNK != 128:
            return weights
        is_first = lax.broadcasted_iota(jnp.int32, (8, HALF), 0) == 0
        last = wide(slice(HALF, HALF + 8))
        return jnp.concatenate([jnp.where(is_first, last, weights[:8]), weights[8:]], axis=0)

    def after_x(parity, x_parity, part, out):
        rows = slice(part * CHUNK, (part + 1) * CHUNK)
        for field in range(2):
            weights = window_block(field, x_parity, parity, part)
            put_rhs(4 + 4 * field + 2 * parity + x_parity, rows, out * weights)

    def inverse_x(field, parity, part):
        slot = 4 + 4 * field + 2 * parity
        return times_left(back_ref[0], slot, part), times_left(back_ref[1], slot + 1, part)

    def after_inverse_x(field, parity, part, out):
        count = CHUNK // 32
        for near in range(2):
            value = out[0] + out[1] if near == 0 else out[0] - out[1]
            high, low = split(value)
            gx = slice(near * 8 + part * count, near * 8 + (part + 1) * count)
            lhs_refs[2 + 2 * field + parity][gx, :, :, :HALF] = high.reshape(count, 2, 16, HALF)
            lhs_refs[2 + 2 * field + parity][gx, :, :, HALF:] = low.reshape(count, 2, 16, HALF)

    def inverse_y(field, part):
        return [times_right(2 + 2 * field + parity, part, table_ref[parity]) for parity in range(2)]

    def finish(field, part, out):
        count = CHUNK // 32
        gx = slice(part * count, (part + 1) * count)
        for near in range(2):
            value = out[0] + out[1] if near == 0 else out[0] - out[1]
            value = value.reshape(count, 2, 16, HALF)
            for pair in range(2):
                cols = slice(pair * 128, (pair + 1) * 128)
                first, second = merge(value[:, 0, :, cols], value[:, 1, :, cols])
                o_ref[gx, 4 * near + 2 * pair, 0, field] = first
                o_ref[gx, 4 * near + 2 * pair + 1, 0, field] = second

    steps = []

    def add(product, use, *where):
        steps.append((lambda: product(*where), lambda out: use(*where, out)))

    for parity in range(2):
        for part in range(parts):
            add(forward_y, after_y, parity, part)
    for parity in range(2):
        for x_parity in range(2):
            for part in range(parts):
                add(forward_x, after_x, parity, x_parity, part)
    for field in range(2):
        for parity in range(2):
            for part in range(parts):
                add(inverse_x, after_inverse_x, field, parity, part)
    for field in range(2):
        for part in range(2 * parts):
            add(inverse_y, finish, field, part)
    loads = [(parity, pair, half) for parity in range(2) for half in range(2) for pair in range(2)]
    for where in loads[:4]:
        load(*where)
    waiting = None
    for index, (product, use) in enumerate(steps):
        out = product()
        if index < parts:
            for where in loads[4 + index * 4 // parts : 4 + (index + 1) * 4 // parts]:
                load(*where)
        if waiting is not None:
            waiting()
        waiting = lambda use=use, out=out: use(out)
    waiting()


def tail_kernel(b_ref, table_ref, o_ref, *scratch):
    lhs_refs, even_ref = scratch[:2], scratch[2]

    def gather(parity, half):
        begin = pl.multiple_of(8 * pl.program_id(1), 8)
        block = b_ref[:, 2 * parity + half, pl.program_id(0), pl.ds(begin, 8), :]
        return jnp.swapaxes(block, 0, 1)

    def put(parity, half, x, value):
        for part, value in enumerate(split(value)):
            start = part * HALF + half * 128
            lhs_refs[parity][x * 128 : (x + 1) * 128, start : start + 128] = value.T

    def transform(parity, x):
        data = lhs_refs[parity][x * 128 : (x + 1) * 128, :]
        data = join(data[:, :HALF], data[:, HALF:], 1)
        return jnp.dot(data, join_table(table_ref[parity], 0), preferred_element_type=F32)

    def store(x, even, odd):
        o_ref[0, :, x, :, :HALF] = (even + odd).reshape(2, 64, HALF)
        o_ref[0, :, x, :, HALF:] = (even - odd).reshape(2, 64, HALF)

    for half in range(2):
        chunks = gather(0, half)
        for x in range(8):
            put(0, half, x, chunks[x])
    for x in range(8):
        even_ref[x] = transform(0, x)
        half = x // 4
        if x % 4 == 0:
            chunks = gather(1, half)
        for y in range(2 * (x % 4), 2 * (x % 4) + 2):
            put(1, half, y, chunks[y])
    waiting = None
    for x in range(8):
        odd = transform(1, x)
        if waiting is not None:
            store(*waiting)
        waiting = (x, even_ref[x], odd)
    store(*waiting)


def window(u_value):
    is_small = u_value < 0.2
    safe_u = jnp.where(is_small, 1.0, u_value)
    closed_form = 3.0 * (jnp.sin(safe_u) - safe_u * jnp.cos(safe_u)) / (safe_u * safe_u * safe_u)
    series = 1.0 - u_value * u_value / 10.0 + u_value**4 / 280.0
    return jnp.where(is_small, series, closed_form)


def plane_windows(radius_cells):
    d = lax.axis_index(AXES)
    kz = jnp.stack([2 * d, jnp.where(d == 0, HALF, 2 * d), 2 * d + 1]).astype(F32)
    even, odd = frequencies()
    rows = np.concatenate([even[:QUARTER], odd[:QUARTER], np.full(8, HALF)])
    cols = np.concatenate([even, odd[:QUARTER]])
    row_squares = jnp.asarray((rows * rows).astype(np.float32))
    col_squares = jnp.asarray((cols * cols).astype(np.float32))
    k_squared = (
        (kz * kz)[:, None, None] + row_squares[None, :, None] + col_squares[None, None, :]
    )
    k_length = 2.0 * math.pi / N * jnp.sqrt(k_squared)
    radius_values = radius_cells.astype(F32)
    return window(k_length[:, None] * radius_values[None, :, None, None])


def whole(shape):
    return pl.BlockSpec(shape, lambda *_: (0,) * len(shape))


TABLE = (2, HALF, N)


def z_forward(density, table):
    return pl.pallas_call(
        head_kernel,
        grid=(2,),
        in_specs=[pl.BlockSpec((2, 8, 64, N), lambda i: (0, i, 0, 0)), whole(TABLE)],
        out_specs=pl.BlockSpec((128, 4, 8, 128), lambda i: (0, 0, i, 0)),
        out_shape=jax.ShapeDtypeStruct((128, 4, 16, 128), F32),
        compiler_params=pltpu.CompilerParams(vmem_limit_bytes=56 * MIB),
    )(density.reshape(2, 16, 64, N), table)


def filter_planes(planes, weights, table, back):
    return pl.pallas_call(
        middle_kernel,
        grid=(4,),
        in_specs=[
            pl.BlockSpec((GX, GY, 1, 16, 128), lambda s: (0, 0, s, 0, 0)),
            pl.BlockSpec((1, 2, HALF + 8, HALF + QUARTER), lambda s: (jnp.minimum(s, 2), 0, 0, 0)),
            pl.BlockSpec(memory_space=pltpu.VMEM),
            pl.BlockSpec(memory_space=pltpu.VMEM),
        ],
        out_specs=pl.BlockSpec((GX, GY, 1, 2, 16, 128), lambda s: (0, 0, s, 0, 0, 0)),
        out_shape=jax.ShapeDtypeStruct((GX, GY, 4, 2, 16, 128), F32),
        scratch_shapes=[
            *[pltpu.VMEM((GX, 2, 16, N), BF16) for _ in range(6)],
            *[pltpu.VMEM((N, HALF), BF16) for _ in range(12)],
        ],
        compiler_params=pltpu.CompilerParams(vmem_limit_bytes=28 * MIB),
    )(planes, weights, table, back)


def z_inverse(filtered, table):
    out = pl.pallas_call(
        tail_kernel,
        grid=(2, 2),
        in_specs=[pl.BlockSpec(memory_space=pltpu.VMEM), pl.BlockSpec(memory_space=pltpu.VMEM)],
        out_specs=pl.BlockSpec((1, 2, 8, 64, N), lambda f, i: (f, 0, i, 0, 0)),
        out_shape=jax.ShapeDtypeStruct((2, 2, 16, 64, N), F32),
        scratch_shapes=[
            *[pltpu.VMEM((1024, N), BF16) for _ in range(2)],
            pltpu.VMEM((8, 128, HALF), F32),
        ],
        compiler_params=pltpu.CompilerParams(vmem_limit_bytes=28 * MIB),
    )(filtered, table)
    return out.reshape(2, 32, 64, N)


def exchange(pieces):
    return lax.all_to_all(pieces, AXES, split_axis=0, concat_axis=0, tiled=True)


def per_device(density, radius_cells):
    table = two_parts(basis())
    back = two_parts(basis().transpose(0, 2, 1))
    planes = exchange(z_forward(density, table))
    weights = plane_windows(radius_cells)
    filtered = filter_planes(planes.reshape(GX, GY, 4, 16, 128), weights, table, back)
    return z_inverse(exchange(filtered.reshape(128, 4, 2, 16, 128)), table)


def solution(mesh):
    return jax.shard_map(
        per_device,
        mesh=mesh,
        in_specs=(P("gx", "gy", None), P()),
        out_specs=P(None, "gx", "gy", None),
        check_vma=False,
    )
```

time: 196 us -> 194 us (0.990)
  Pallas kernels: 29 us -> 26.8 us
where the time goes in v3:
time: 194 us
  blocking collectives  103 us (53%)
  waiting for transfers between devices  42.1 us (22%)
  Pallas kernels  26.8 us (14%)
  starting transfers between devices  12 us (6%)
  other arithmetic  10.3 us (5%)
    all_to_all x1, blocking collectives, exchange(): return lax.all_to_all(pieces, AXES, split_axis=0, concat_axis=0, tiled=True)  103 us
    all_to_all x1, waiting for transfers between devices, exchange(): return lax.all_to_all(pieces, AXES, split_axis=0, concat_axis=0, tiled=True)  42.1 us
    pallas_call x1, Pallas kernels, filter_planes(): pl.pallas_call(middle_kernel, grid=(4,), in_specs=[pl.BlockSpec((GX, GY,...  13.7 us
    all_to_all x1, starting transfers between devices, exchange(): return lax.all_to_all(pieces, AXES, split_axis=0, concat_axis=0, tiled=True)  12 us
    select_n x1, other arithmetic, window(): return jnp.where(is_small, series, closed_form)  9.71 us
    pallas_call x1, Pallas kernels, z_inverse(): pl.pallas_call(tail_kernel, grid=(2, 2), in_specs=[pl.BlockSpec(memory_sp...  7.54 us
    pallas_call x1, Pallas kernels, z_forward(): pl.pallas_call(head_kernel, grid=(2,), in_specs=[pl.BlockSpec((2, 8, 64,...  5.63 us
  transfers between devices with their start and end apart: 1, of which 1 were waited for; matrix products, arithmetic and copies ran while one was open for 5% of the time, Pallas kernels for 0%

profile of v3, /device:TPU:1, one launch (start us, length us, event | category | flops | bytes accessed | tf_op | source)
XLA Modules:
  0.0 193.9 jit_solution(14317368227189087207)
XLA Ops:
  0.0 5.6 %shard_map.64 = f32[128,4,16,128]{3,2,1,0:T(8,128)} custom-call(f32[2,16,64,512]{3,2,1,0:T(8,128)} %bitcast.8, bf16[2,256,512]{2,1,0:T(8,128)(2,1)} %constant.42.clone.table_ref), custom_call_target="tpu_custom_call" | custom-call | tf_op jit(solution)/shard_map/pallas_call | solution.py:293
  5.6 0.0 copy-start.4
  5.6 0.0 copy-start.3
  5.6 0.0 copy-start.2
  5.6 12.0 %all-to-all-start = ((f32[128,4,16,128]{3,2,1,0:T(8,128)}), f32[128,4,16,128]{3,2,1,0:T(8,128)}, u32[]{:S(2)}, u32[]{:S(2)}) async-start(f32[128,4,16,128]{3,2,1,0:T(8,128)} %shard_map.64), calls=%async_computation | async-start | bytes 8388608 | tf_op jit(solution)/shard_map/all_to_all | solution.py:340
  17.6 0.0 copy-done.4
  17.6 0.1 fusion.14
  17.7 0.0 copy-done.3
  17.7 0.1 broadcast_add_fusion
  17.8 0.0 copy-done.2
  17.8 0.0 copy-start
  17.8 0.0 copy-start.1
  17.8 0.4 sqrt_multiply_fusion
  18.2 9.7 %fusion.7.w_ref = f32[3,2,264,384]{3,2,1,0:T(8,128)S(1)} fusion(f32[2]{0:T(128)S(1)} %convert_element_type.11, f32[3,264,384]{2,1,0:T(8,128)S(1)} %sqrt_multiply_fusion), kind=kLoop, calls=%fused_computation.10 | loop fusion | flops 9732096 | bytes 3649544 | tf_op jit(solution)/shard_map/jit(_where)/select_n | solution.py:266
  28.0 42.1 %all-to-all-done = f32[128,4,16,128]{3,2,1,0:T(8,128)} async-done(((f32[128,4,16,128]{3,2,1,0:T(8,128)}), f32[128,4,16,128]{3,2,1,0:T(8,128)}, u32[]{:S(2)}, u32[]{:S(2)}) %all-to-all-start) | async-done | bytes 4194336 | tf_op jit(solution)/shard_map/all_to_all | solution.py:340
  70.0 0.0 copy-done
  70.0 0.0 copy-done.1
  70.0 13.7 %shard_map.65 = f32[16,8,4,2,16,128]{5,4,3,2,1,0:T(8,128)S(1)} custom-call(f32[16,8,4,16,128]{4,3,2,1,0:T(8,128)} %bitcast.1.r_ref, f32[3,2,264,384]{3,2,1,0:T(8,128)S(1)} %fusion.7.w_ref, bf16[2,256,512]{2,1,0:T(8,128)(2,1)S(1)} %copy-done, bf16[2,256,512]{2,1,0:T(8,128)(2,1)S(1)} %copy-done.1), custom_call_target="tpu_custom_call" | custom-call | tf_op jit(solution)/shard_map/pallas_call | solution.py:304
  83.7 102.6 %all_to_all.10.b_ref = f32[128,4,2,16,128]{4,3,2,1,0:T(8,128)S(1)} all-to-all(f32[128,4,2,16,128]{4,3,2,1,0:T(8,128)S(1)} %bitcast.7), channel_id=1, replica_groups=mesh['gx'=16,'gy'=8] {'gx','gy'}, dimensions={0} | all-to-all | bytes 16777216 | tf_op jit(solution)/shard_map/all_to_all | solution.py:340
  186.3 7.5 %shard_map.66 = f32[2,2,16,64,512]{4,3,2,1,0:T(8,128)} custom-call(f32[128,4,2,16,128]{4,3,2,1,0:T(8,128)S(1)} %all_to_all.10.b_ref, bf16[2,256,512]{2,1,0:T(8,128)(2,1)S(1)} %copy-done), custom_call_target="tpu_custom_call" | custom-call | tf_op jit(solution)/shard_map/pallas_call | solution.py:324
  (1 shorter events, 0.0 us)
Async XLA Ops:
  5.6 12.0 %copy-start.4 = (s32[2]{0:T(128)S(1)}, s32[2]{0:T(128)}, u32[]{:S(2)}) copy-start(s32[2]{0:T(128)} %param.7) | copy-start | bytes 28
  5.6 12.1 %copy-start.3 = (f32[264]{0:T(512)S(1)}, f32[264]{0:T(512)}, u32[]{:S(2)}) copy-start(f32[264]{0:T(512)} %constant.44.clone) | copy-start | bytes 3172
  5.6 12.2 %copy-start.2 = (f32[384]{0:T(512)S(1)}, f32[384]{0:T(512)}, u32[]{:S(2)}) copy-start(f32[384]{0:T(512)} %constant.45.clone) | copy-start | bytes 4612
  5.6 64.4 %all-to-all-start = ((f32[128,4,16,128]{3,2,1,0:T(8,128)}), f32[128,4,16,128]{3,2,1,0:T(8,128)}, u32[]{:S(2)}, u32[]{:S(2)}) async-start(f32[128,4,16,128]{3,2,1,0:T(8,128)} %shard_map.64), calls=%async_computation | async-start | bytes 8388608 | tf_op jit(solution)/shard_map/all_to_all | solution.py:340
  17.8 52.2 %copy-start = (bf16[2,256,512]{2,1,0:T(8,128)(2,1)S(1)}, bf16[2,256,512]{2,1,0:T(8,128)(2,1)}, u32[]{:S(2)}) copy-start(bf16[2,256,512]{2,1,0:T(8,128)(2,1)} %constant.42.clone.table_ref) | copy-start | bytes 1572868
  17.8 52.2 %copy-start.1 = (bf16[2,256,512]{2,1,0:T(8,128)(2,1)S(1)}, bf16[2,256,512]{2,1,0:T(8,128)(2,1)}, u32[]{:S(2)}) copy-start(bf16[2,256,512]{2,1,0:T(8,128)(2,1)} %constant.43.clone.back_ref) | copy-start | bytes 1572868

commit v4 on v3

--- a/solution.py
+++ b/solution.py
@@ -216,46 +216,63 @@
     waiting()
 
 
-def tail_kernel(b_ref, table_ref, o_ref, *scratch):
-    lhs_refs, even_ref = scratch[:2], scratch[2]
-
-    def gather(parity, half):
-        begin = pl.multiple_of(8 * pl.program_id(1), 8)
-        block = b_ref[:, 2 * parity + half, pl.program_id(0), pl.ds(begin, 8), :]
-        return jnp.swapaxes(block, 0, 1)
-
-    def put(parity, half, x, value):
+def tail_kernel(b_ref, table_ref, o_ref, stage_ref, done, *scratch):
+    lhs_refs, even_refs = scratch[:4], scratch[4:]
+
+    def gather(block, parity, half):
+        rows = slice(8 * (block % 2), 8 * (block % 2) + 8)
+        return jnp.swapaxes(b_ref[:, 2 * parity + half, block // 2, rows, :], 0, 1)
+
+    def put(block, parity, half, x, value):
         for part, value in enumerate(split(value)):
             start = part * HALF + half * 128
-            lhs_refs[parity][x * 128 : (x + 1) * 128, start : start + 128] = value.T
-
-    def transform(parity, x):
-        data = lhs_refs[parity][x * 128 : (x + 1) * 128, :]
+            rows = slice(x * 128, (x + 1) * 128)
+            lhs_refs[2 * (block % 2) + parity][rows, start : start + 128] = value.T
+
+    def transform(block, parity, x):
+        data = lhs_refs[2 * (block % 2) + parity][x * 128 : (x + 1) * 128, :]
         data = join(data[:, :HALF], data[:, HALF:], 1)
         return jnp.dot(data, join_table(table_ref[parity], 0), preferred_element_type=F32)
 
-    def store(x, even, odd):
-        o_ref[0, :, x, :, :HALF] = (even + odd).reshape(2, 64, HALF)
-        o_ref[0, :, x, :, HALF:] = (even - odd).reshape(2, 64, HALF)
-
-    for half in range(2):
-        chunks = gather(0, half)
+    def send(block, x):
+        return pltpu.make_async_copy(
+            stage_ref.at[block, x],
+            o_ref.at[block // 2, :, 8 * (block % 2) + x],
+            done.at[8 * block + x],
+        )
+
+    def store(block, x, even, odd):
+        stage_ref[block, x, :, :, :HALF] = (even + odd).reshape(2, 64, HALF)
+        stage_ref[block, x, :, :, HALF:] = (even - odd).reshape(2, 64, HALF)
+        send(block, x).start()
+
+    waiting = None
+    for block in range(4):
+        for half in range(2):
+            chunks = gather(block, 0, half)
+            for x in range(8):
+                put(block, 0, half, x, chunks[x])
+        for parity in range(2):
+            for x in range(8):
+                out = transform(block, parity, x)
+                following = (block, 1)
+                if parity == 0:
+                    half = x // 4
+                    if x % 4 == 0:
+                        chunks = gather(*following, half)
+                    for y in range(2 * (x % 4), 2 * (x % 4) + 2):
+                        put(*following, half, y, chunks[y])
+                if waiting is not None:
+                    store(*waiting)
+                    waiting = None
+                if parity == 0:
+                    even_refs[block % 2][x] = out
+                else:
+                    waiting = (block, x, even_refs[block % 2][x], out)
+    store(*waiting)
+    for block in range(4):
         for x in range(8):
-            put(0, half, x, chunks[x])
-    for x in range(8):
-        even_ref[x] = transform(0, x)
-        half = x // 4
-        if x % 4 == 0:
-            chunks = gather(1, half)
-        for y in range(2 * (x % 4), 2 * (x % 4) + 2):
-            put(1, half, y, chunks[y])
-    waiting = None
-    for x in range(8):
-        odd = transform(1, x)
-        if waiting is not None:
-            store(*waiting)
-        waiting = (x, even_ref[x], odd)
-    store(*waiting)
+            send(block, x).wait()
 
 
 def window(u_value):
@@ -323,13 +340,14 @@
 def z_inverse(filtered, table):
     out = pl.pallas_call(
         tail_kernel,
-        grid=(2, 2),
         in_specs=[pl.BlockSpec(memory_space=pltpu.VMEM), pl.BlockSpec(memory_space=pltpu.VMEM)],
-        out_specs=pl.BlockSpec((1, 2, 8, 64, N), lambda f, i: (f, 0, i, 0, 0)),
+        out_specs=pl.BlockSpec(memory_space=pl.ANY),
         out_shape=jax.ShapeDtypeStruct((2, 2, 16, 64, N), F32),
         scratch_shapes=[
-            *[pltpu.VMEM((1024, N), BF16) for _ in range(2)],
-            pltpu.VMEM((8, 128, HALF), F32),
+            pltpu.VMEM((4, 8, 2, 64, N), F32),
+            pltpu.SemaphoreType.DMA((32,)),
+            *[pltpu.VMEM((1024, N), BF16) for _ in range(4)],
+            *[pltpu.VMEM((8, 128, HALF), F32) for _ in range(2)],
         ],
         compiler_params=pltpu.CompilerParams(vmem_limit_bytes=28 * MIB),
     )(filtered, table)

time: 194 us -> 194 us (level)
  no operation moved by 1% of the time
where the time goes in v4:
time: 194 us
  blocking collectives  103 us (53%)
  waiting for transfers between devices  42.1 us (22%)
  Pallas kernels  26.5 us (14%)
  starting transfers between devices  12 us (6%)
  other arithmetic  10.3 us (5%)
    all_to_all x1, blocking collectives, exchange(): return lax.all_to_all(pieces, AXES, split_axis=0, concat_axis=0, tiled=True)  103 us
    all_to_all x1, waiting for transfers between devices, exchange(): return lax.all_to_all(pieces, AXES, split_axis=0, concat_axis=0, tiled=True)  42.1 us
    pallas_call x1, Pallas kernels, filter_planes(): pl.pallas_call(middle_kernel, grid=(4,), in_specs=[pl.BlockSpec((GX, GY,...  13.7 us
    all_to_all x1, starting transfers between devices, exchange(): return lax.all_to_all(pieces, AXES, split_axis=0, concat_axis=0, tiled=True)  12 us
    select_n x1, other arithmetic, window(): return jnp.where(is_small, series, closed_form)  9.71 us
    pallas_call x1, Pallas kernels, z_inverse(): pl.pallas_call(tail_kernel, in_specs=[pl.BlockSpec(memory_space=pltpu.VME...  7.18 us
    pallas_call x1, Pallas kernels, z_forward(): pl.pallas_call(head_kernel, grid=(2,), in_specs=[pl.BlockSpec((2, 8, 64,...  5.63 us
  transfers between devices with their start and end apart: 1, of which 1 were waited for; matrix products, arithmetic and copies ran while one was open for 5% of the time, Pallas kernels for 0%

profile of v4, /device:TPU:1, one launch (start us, length us, event | category | flops | bytes accessed | tf_op | source)
XLA Modules:
  0.0 193.7 jit_solution(12677000831464726136)
XLA Ops:
  0.0 5.6 %shard_map.64 = f32[128,4,16,128]{3,2,1,0:T(8,128)} custom-call(f32[2,16,64,512]{3,2,1,0:T(8,128)} %bitcast.8, bf16[2,256,512]{2,1,0:T(8,128)(2,1)} %constant.42.clone.table_ref), custom_call_target="tpu_custom_call" | custom-call | tf_op jit(solution)/shard_map/pallas_call | solution.py:310
  5.6 0.0 copy-start.4
  5.6 0.0 copy-start.3
  5.6 0.0 copy-start.2
  5.6 12.0 %all-to-all-start = ((f32[128,4,16,128]{3,2,1,0:T(8,128)}), f32[128,4,16,128]{3,2,1,0:T(8,128)}, u32[]{:S(2)}, u32[]{:S(2)}) async-start(f32[128,4,16,128]{3,2,1,0:T(8,128)} %shard_map.64), calls=%async_computation | async-start | bytes 8388608 | tf_op jit(solution)/shard_map/all_to_all | solution.py:358
  17.6 0.0 copy-done.4
  17.6 0.1 fusion.14
  17.7 0.0 copy-done.3
  17.7 0.1 broadcast_add_fusion
  17.8 0.0 copy-done.2
  17.8 0.0 copy-start
  17.8 0.0 copy-start.1
  17.8 0.4 sqrt_multiply_fusion
  18.2 9.7 %fusion.7.w_ref = f32[3,2,264,384]{3,2,1,0:T(8,128)S(1)} fusion(f32[2]{0:T(128)S(1)} %convert_element_type.11, f32[3,264,384]{2,1,0:T(8,128)S(1)} %sqrt_multiply_fusion), kind=kLoop, calls=%fused_computation.10 | loop fusion | flops 9732096 | bytes 3649544 | tf_op jit(solution)/shard_map/jit(_where)/select_n | solution.py:283
  28.0 42.1 %all-to-all-done = f32[128,4,16,128]{3,2,1,0:T(8,128)} async-done(((f32[128,4,16,128]{3,2,1,0:T(8,128)}), f32[128,4,16,128]{3,2,1,0:T(8,128)}, u32[]{:S(2)}, u32[]{:S(2)}) %all-to-all-start) | async-done | bytes 4194336 | tf_op jit(solution)/shard_map/all_to_all | solution.py:358
  70.0 0.0 copy-done
  70.0 0.0 copy-done.1
  70.0 13.7 %shard_map.65 = f32[16,8,4,2,16,128]{5,4,3,2,1,0:T(8,128)S(1)} custom-call(f32[16,8,4,16,128]{4,3,2,1,0:T(8,128)} %bitcast.1.r_ref, f32[3,2,264,384]{3,2,1,0:T(8,128)S(1)} %fusion.7.w_ref, bf16[2,256,512]{2,1,0:T(8,128)(2,1)S(1)} %copy-done, bf16[2,256,512]{2,1,0:T(8,128)(2,1)S(1)} %copy-done.1), custom_call_target="tpu_custom_call" | custom-call | tf_op jit(solution)/shard_map/pallas_call | solution.py:321
  83.7 102.6 %all_to_all.10.b_ref = f32[128,4,2,16,128]{4,3,2,1,0:T(8,128)S(1)} all-to-all(f32[128,4,2,16,128]{4,3,2,1,0:T(8,128)S(1)} %bitcast.7), channel_id=1, replica_groups=mesh['gx'=16,'gy'=8] {'gx','gy'}, dimensions={0} | all-to-all | bytes 16777216 | tf_op jit(solution)/shard_map/all_to_all | solution.py:358
  186.3 7.2 %shard_map.66 = f32[2,2,16,64,512]{4,3,2,1,0:T(8,128)} custom-call(f32[128,4,2,16,128]{4,3,2,1,0:T(8,128)S(1)} %all_to_all.10.b_ref, bf16[2,256,512]{2,1,0:T(8,128)(2,1)S(1)} %copy-done), custom_call_target="tpu_custom_call" | custom-call | tf_op jit(solution)/shard_map/pallas_call | solution.py:341
  (1 shorter events, 0.0 us)
Async XLA Ops:
  5.6 12.0 %copy-start.4 = (s32[2]{0:T(128)S(1)}, s32[2]{0:T(128)}, u32[]{:S(2)}) copy-start(s32[2]{0:T(128)} %param.7) | copy-start | bytes 28
  5.6 12.1 %copy-start.3 = (f32[264]{0:T(512)S(1)}, f32[264]{0:T(512)}, u32[]{:S(2)}) copy-start(f32[264]{0:T(512)} %constant.44.clone) | copy-start | bytes 3172
  5.6 12.2 %copy-start.2 = (f32[384]{0:T(512)S(1)}, f32[384]{0:T(512)}, u32[]{:S(2)}) copy-start(f32[384]{0:T(512)} %constant.45.clone) | copy-start | bytes 4612
  5.6 64.4 %all-to-all-start = ((f32[128,4,16,128]{3,2,1,0:T(8,128)}), f32[128,4,16,128]{3,2,1,0:T(8,128)}, u32[]{:S(2)}, u32[]{:S(2)}) async-start(f32[128,4,16,128]{3,2,1,0:T(8,128)} %shard_map.64), calls=%async_computation | async-start | bytes 8388608 | tf_op jit(solution)/shard_map/all_to_all | solution.py:358
  17.8 52.2 %copy-start = (bf16[2,256,512]{2,1,0:T(8,128)(2,1)S(1)}, bf16[2,256,512]{2,1,0:T(8,128)(2,1)}, u32[]{:S(2)}) copy-start(bf16[2,256,512]{2,1,0:T(8,128)(2,1)} %constant.42.clone.table_ref) | copy-start | bytes 1572868
  17.8 52.2 %copy-start.1 = (bf16[2,256,512]{2,1,0:T(8,128)(2,1)S(1)}, bf16[2,256,512]{2,1,0:T(8,128)(2,1)}, u32[]{:S(2)}) copy-start(bf16[2,256,512]{2,1,0:T(8,128)(2,1)} %constant.43.clone.back_ref) | copy-start | bytes 1572868
